TPU v7x, 32 devices: a whole 2x2x4 slice. The times are simulated.
32 devices in a mesh: seq: 2 (over x), shard: 16 (over z, y, core).
Axes of the slice: x: 2, y: 2, z: 4, core: 2. Of those that a mesh axis runs over, the one named last changes fastest.
Arguments:
- tokens: bfloat16 [16, 320, 2048], P('shard', 'seq'), may hold values from -6 to 6
- cotangent: bfloat16 [16, 320, 2048], P('shard', 'seq'), may hold values from -6 to 6
- norm1_gain: bfloat16 [2048], P(('seq', 'shard')), may hold values from 0.25 to 1.75
- norm1_bias: bfloat16 [2048], P(('seq', 'shard')), may hold values from -3 to 3
- qkv_weight: bfloat16 [2048, 6144], P(('seq', 'shard')), may hold values from -0.125 to 0.125
- qkv_bias: bfloat16 [6144], P(('seq', 'shard')), may hold values from -3 to 3
- out_weight: bfloat16 [2048, 2048], P(('seq', 'shard')), may hold values from -0.5 to 0.5
- norm2_gain: bfloat16 [2048], P(('seq', 'shard')), may hold values from 0.25 to 1.75
- norm2_bias: bfloat16 [2048], P(('seq', 'shard')), may hold values from -3 to 3
- gate_weight: bfloat16 [2048, 5632], P(('seq', 'shard')), may hold values from -0.125 to 0.125
- up_weight: bfloat16 [2048, 5632], P(('seq', 'shard')), may hold values from -0.125 to 0.125
- down_weight: bfloat16 [5632, 2048], P(('seq', 'shard')), may hold values from -0.078125 to 0.078125
Outputs:
- out: bfloat16 [16, 320, 2048], P('shard', 'seq')
- d_input: float32 [16, 320, 2048], P('shard', 'seq')
- norm1_gain_grad: float32 [2048], P(('seq', 'shard'))
- norm1_bias_grad: float32 [2048], P(('seq', 'shard'))
- qkv_weight_grad: float32 [2048, 6144], P(('seq', 'shard'))
- qkv_bias_grad: float32 [6144], P(('seq', 'shard'))
- out_weight_grad: float32 [2048, 2048], P(('seq', 'shard'))
- norm2_gain_grad: float32 [2048], P(('seq', 'shard'))
- norm2_bias_grad: float32 [2048], P(('seq', 'shard'))
- gate_weight_grad: float32 [2048, 5632], P(('seq', 'shard'))
- up_weight_grad: float32 [2048, 5632], P(('seq', 'shard'))
- down_weight_grad: float32 [5632, 2048], P(('seq', 'shard'))
All inputs are finite; a program needn't handle non-finite values.
Results may differ from a plain program's by a relative error of at most 0.012.
Values may be sent and summed in bfloat16 or wider, within the bound.
A program may use at most 448 MiB of HBM per device.

v0:
```python
import jax
import jax.numpy as jnp
import numpy as np
from jax import lax
from jax.experimental import pallas as pl
from jax.experimental.pallas import tpu as pltpu
from jax.sharding import PartitionSpec as P

HEADS = 32
HEAD_DIM = 64
ROTARY = 16
TEAM = ("seq", "zl")
PEERS = ("zh", "y", "c")
ALL = ("seq", "zh", "zl", "y", "c")
BF = jnp.bfloat16
F32 = jnp.float32


def norm_rows(values):
    centre = jnp.mean(values, axis=-1, keepdims=True)
    centred = values - centre
    spread = jnp.mean(centred * centred, axis=-1, keepdims=True)
    scale_rows = lax.rsqrt(spread + 1e-05)
    return (centred * scale_rows, scale_rows)


def norm_back(grad_normed, normed, scale_rows):
    return scale_rows * (
        grad_normed
        - jnp.mean(grad_normed, axis=-1, keepdims=True)
        - normed * jnp.mean(grad_normed * normed, axis=-1, keepdims=True)
    )


def rotate(values, positions, direction):
    halves = ROTARY // 2
    frequency = 10000.0 ** (-2.0 * jnp.arange(halves, dtype=F32) / ROTARY)
    angles = positions.astype(F32)[:, None] * frequency[None, :]
    cosine_table = jnp.cos(angles)[:, None, :]
    sine_table = jnp.sin(angles)[:, None, :] * direction
    first_half = values[..., :halves]
    second_half = values[..., halves:ROTARY]
    return jnp.concatenate(
        [
            first_half * cosine_table - second_half * sine_table,
            second_half * cosine_table + first_half * sine_table,
            values[..., ROTARY:],
        ],
        axis=-1,
    )


def dot(left, right):
    return jnp.dot(left, right, preferred_element_type=F32)


def dot_nt(left, right):
    return lax.dot_general(left, right, (((1,), (1,)), ((), ())), preferred_element_type=F32)


def dot_tn(left, right):
    return lax.dot_general(left, right, (((0,), (0,)), ((), ())), preferred_element_type=F32)


def plain_device(
    tokens, cotangent, norm1_gain, norm1_bias, qkv_weight, qkv_bias, out_weight,
    norm2_gain, norm2_bias, gate_weight, up_weight, down_weight,
):
    zh = lax.axis_size("zh")
    rows = tokens.shape[1]
    width = tokens.shape[2]
    own = qkv_weight.shape[0]
    ff = gate_weight.shape[1]
    half = lax.axis_size("seq")
    length = rows * half
    team = half * lax.axis_size("zl")
    seqs = lax.axis_size("zl")

    def cut_columns(shard, parts):
        block = shard.shape[1] // parts // (half * zh * seqs)
        cut = shard.reshape(own, parts, half, zh, seqs, block).transpose(2, 4, 0, 1, 3, 5)
        return cut.reshape(team, own, parts * zh * block)

    def join_columns(cut, parts):
        block = cut.shape[2] // parts // zh
        cut = cut.reshape(half, seqs, own, parts, zh, block).transpose(2, 3, 0, 4, 1, 5)
        return cut.reshape(own, -1)

    def mine_columns(whole, parts):
        block = whole.shape[0] // parts // (half * zh * seqs)
        cut = whole.reshape(parts, half, zh, seqs, block)
        cut = lax.dynamic_index_in_dim(cut, lax.axis_index("seq"), 1, keepdims=False)
        cut = lax.dynamic_index_in_dim(cut, lax.axis_index("zl"), 2, keepdims=False)
        return cut.reshape(-1)

    def to_owner_order(values):
        n = values.shape[0]
        return values.reshape(n, half, zh, seqs, 4, own).transpose(0, 2, 4, 1, 3, 5).reshape(n, width)

    def from_owner_order(values):
        n = values.shape[0]
        return values.reshape(n, zh, 4, half, seqs, own).transpose(0, 3, 1, 4, 2, 5).reshape(n, width)

    def gather_columns(shard, parts):
        cut = cut_columns(shard, parts)
        cut = lax.all_to_all(cut, TEAM, split_axis=0, concat_axis=0, tiled=True)
        return lax.all_gather(cut.reshape(team * own, -1), PEERS, axis=0, tiled=True)

    def gather_rows(shard):
        return lax.all_gather(shard, PEERS, axis=0, tiled=True)

    def gather_tokens(values):
        return lax.all_gather(values, ("zl", "seq"), axis=0, tiled=True)

    def sum_tokens(values):
        return lax.psum_scatter(values.astype(BF), ("zl", "seq"), scatter_dimension=0, tiled=True).astype(F32)

    def sum_rows(values):
        return lax.psum_scatter(values.astype(BF), PEERS, scatter_dimension=0, tiled=True)

    def sum_columns(values, parts):
        part = sum_rows(values).reshape(team, own, -1)
        part = lax.all_to_all(part, TEAM, split_axis=0, concat_axis=0, tiled=True)
        return join_columns(part, parts).astype(F32)

    small = jnp.concatenate([norm1_gain, norm1_bias, norm2_gain, norm2_bias, qkv_bias])
    small = lax.all_gather(small, ALL, axis=0, tiled=False)
    first_gain = small[:, :own].reshape(-1).astype(F32)
    first_bias = small[:, own : 2 * own].reshape(-1).astype(F32)
    second_gain = small[:, 2 * own : 3 * own].reshape(-1).astype(F32)
    second_bias = small[:, 3 * own : 4 * own].reshape(-1).astype(F32)
    qkv_offset = mine_columns(small[:, 4 * own :].reshape(-1), 3).astype(F32)

    inputs = tokens[0].astype(F32)
    first_normed, first_scale = norm_rows(inputs)
    first_own = to_owner_order((first_normed * first_gain + first_bias).astype(BF))
    first_input = gather_tokens(first_own)
    qkv_matrix = gather_columns(qkv_weight, 3)
    out_matrix = gather_rows(out_weight)
    gate_matrix = gather_columns(gate_weight, 1)
    up_matrix = gather_columns(up_weight, 1)
    down_matrix = gather_rows(down_weight)
    upstream = gather_tokens(cotangent[0])

    projected = dot(first_input, qkv_matrix) + qkv_offset
    part = width // team
    group_heads = part // HEAD_DIM
    positions = jnp.tile(jnp.arange(length, dtype=jnp.int32), seqs)

    def heads_of(values):
        return values.reshape(seqs, length, group_heads, HEAD_DIM).transpose(0, 2, 1, 3)

    def unheads(values):
        return values.transpose(0, 2, 1, 3).reshape(seqs * length, part)

    queries = heads_of(rotate(projected[:, :part].reshape(-1, group_heads, HEAD_DIM), positions, 1.0).astype(BF))
    keys = heads_of(rotate(projected[:, part : 2 * part].reshape(-1, group_heads, HEAD_DIM), positions, 1.0).astype(BF))
    values = heads_of(projected[:, 2 * part :].astype(BF))
    causal = jnp.arange(length)[:, None] >= jnp.arange(length)[None, :]
    scores = jnp.einsum("shqd,shkd->shqk", queries, keys, preferred_element_type=F32) * 0.125
    scores = jnp.where(causal, scores, -1e30)
    highest = jnp.max(scores, axis=-1, keepdims=True)
    exponent = jnp.exp(scores - highest)
    probs = exponent / jnp.sum(exponent, axis=-1, keepdims=True)
    probs_low = probs.astype(BF)
    mixed = unheads(jnp.einsum("shqk,shkd->shqd", probs_low, values, preferred_element_type=F32).astype(BF))
    middle = inputs + sum_tokens(dot(mixed, out_matrix))

    second_normed, second_scale = norm_rows(middle)
    second_own = to_owner_order((second_normed * second_gain + second_bias).astype(BF))
    second_input = gather_tokens(second_own)
    gate_rows = dot(second_input, gate_matrix)
    up_rows = dot(second_input, up_matrix)
    sigmoid_gate = jax.nn.sigmoid(gate_rows)
    silu_gate = gate_rows * sigmoid_gate
    hidden = (silu_gate * up_rows).astype(BF)
    result = middle + sum_tokens(dot(hidden, down_matrix))

    down_total = sum_rows(dot_tn(hidden, upstream)).astype(F32)
    grad_hidden = dot_nt(upstream, down_matrix)
    grad_gate = (grad_hidden * up_rows * sigmoid_gate * (1.0 + gate_rows * (1.0 - sigmoid_gate))).astype(BF)
    grad_up = (grad_hidden * silu_gate).astype(BF)
    gate_total = sum_columns(dot_tn(second_input, grad_gate), 1)
    up_total = sum_columns(dot_tn(second_input, grad_up), 1)
    grad_second = from_owner_order(sum_tokens(dot_nt(grad_gate, gate_matrix) + dot_nt(grad_up, up_matrix)))
    grad_middle = cotangent[0].astype(F32) + norm_back(grad_second * second_gain, second_normed, second_scale)
    grad_attended = gather_tokens(grad_middle.astype(BF))
    out_total = sum_rows(dot_tn(mixed, grad_attended)).astype(F32)
    grad_mixed = heads_of(dot_nt(grad_attended, out_matrix).astype(BF))
    grad_probs = jnp.einsum("shqd,shkd->shqk", grad_mixed, values, preferred_element_type=F32)
    grad_scores = (probs * (grad_probs - jnp.sum(probs * grad_probs, axis=-1, keepdims=True))).astype(BF)
    grad_queries = (jnp.einsum("shqk,shkd->shqd", grad_scores, keys, preferred_element_type=F32) * 0.125).astype(BF)
    grad_keys = (jnp.einsum("shqk,shqd->shkd", grad_scores, queries, preferred_element_type=F32) * 0.125).astype(BF)
    grad_values = jnp.einsum("shqk,shqd->shkd", probs_low, grad_mixed, preferred_element_type=F32).astype(BF)
    grad_queries = rotate(unheads(grad_queries).astype(F32).reshape(-1, group_heads, HEAD_DIM), positions, -1.0)
    grad_keys = rotate(unheads(grad_keys).astype(F32).reshape(-1, group_heads, HEAD_DIM), positions, -1.0)
    grad_projected = jnp.concatenate(
        [grad_queries.reshape(-1, part).astype(BF), grad_keys.reshape(-1, part).astype(BF), unheads(grad_values)],
        axis=1,
    )
    qkv_total = sum_columns(dot_tn(first_input, grad_projected), 3)
    grad_first = from_owner_order(sum_tokens(dot_nt(grad_projected, qkv_matrix)))
    grad_inputs = grad_middle + norm_back(grad_first * first_gain, first_normed, first_scale)

    bias_part = jnp.sum(grad_projected.astype(F32), axis=0).reshape(3, zh, -1)
    bias_whole = jnp.zeros((3, half, zh, seqs, bias_part.shape[2]), F32)
    bias_whole = lax.dynamic_update_slice(
        bias_whole, bias_part[:, None, :, None], (0, lax.axis_index("seq"), 0, lax.axis_index("zl"), 0)
    ).reshape(-1)
    count = width // own
    sums = jnp.concatenate(
        [
            jnp.sum(grad_first * first_normed, axis=0).reshape(count, own),
            jnp.sum(grad_first, axis=0).reshape(count, own),
            jnp.sum(grad_second * second_normed, axis=0).reshape(count, own),
            jnp.sum(grad_second, axis=0).reshape(count, own),
            bias_whole.reshape(count, 3 * own),
        ],
        axis=1,
    )
    sums = lax.psum_scatter(sums, ALL, scatter_dimension=0, tiled=True)[0]
    return (
        result.astype(BF)[None],
        grad_inputs[None],
        sums[:own],
        sums[own : 2 * own],
        qkv_total,
        sums[4 * own :],
        out_total,
        sums[2 * own : 3 * own],
        sums[3 * own : 4 * own],
        gate_total,
        up_total,
        down_total,
    )


MESH = pl.DeviceIdType.MESH
ROWS = 16
QKV_PARTS, QKV_GATHERS, OUT_PARTS, FF_PARTS, DOWN_PARTS = 2, 3, 2, 2, 4


class Place:
    def __init__(self, zhs):
        self.s, self.zh, self.zl, self.y, self.c = (lax.axis_index(axis) for axis in ALL)
        self.zhs = zhs

    def at(self, **changed):
        return tuple(changed.get(name, getattr(self, name)) for name in ("s", "zh", "zl", "y", "c"))

    def mates(self):
        for flip_s, flip_z in ((0, 1), (1, 0), (1, 1)):
            yield (1 - self.s if flip_s else self.s), (1 - self.zl if flip_z else self.zl)

    def highs(self):
        for step in range(1, self.zhs):
            yield (self.zh + step) % self.zhs

    def greet(self):
        partners = [self.at(s=s, zl=zl) for s, zl in self.mates()]
        partners += [self.at(zh=zh) for zh in self.highs()]
        partners += [self.at(y=1 - self.y), self.at(c=1 - self.c)]
        barrier = pltpu.get_barrier_semaphore()
        for partner in partners:
            pl.semaphore_signal(barrier, inc=1, device_id=partner, device_id_type=MESH)
        pl.semaphore_wait(barrier, len(partners))


class Traffic:
    def __init__(self):
        self.now, self.active = 0.0, []

    def start(self, demands):
        transfer = {"left": {link: time for link, time in demands.items()}, "done": None}
        self.active.append(transfer)
        return transfer

    def backlog(self, link):
        return sum(transfer["left"].get(link, 0.0) for transfer in self.active)

    def advance(self, until):
        while self.now < until:
            shares = {}
            for transfer in self.active:
                for link in transfer["left"]:
                    shares[link] = shares.get(link, 0) + 1
            step = until - self.now
            for transfer in self.active:
                for link, left in transfer["left"].items():
                    step = min(step, left * shares[link])
            self.now += step
            for transfer in list(self.active):
                transfer["left"] = {
                    link: left - step / shares[link]
                    for link, left in transfer["left"].items()
                    if left - step / shares[link] > 1e-6
                }
                if not transfer["left"]:
                    transfer["done"] = self.now + LATENCY
                    self.active.remove(transfer)


LATENCY = 2.0
ENTER_PLAN = {"small": (7.8, 43), "qkv0": (4.3, 33), "qkv1": (10.8, 0), "qkv2": (6.1, 1), "qkv3": (10.6, 19), "qkv4": (3.8, 13), "qkv5": (11.5, 41), "out0": (2.2, 0), "out1": (2.6, 32), "tokens": (5.8, 13), "cut": (7, 0)}
MIDDLE_PLAN = {"tokens": (0, 0), "ff0": (1, 0), "ff1": (3, 0), "ff2": (4, 0), "ff3": (5, 0), "ff4": (6, 0), "ff5": (7, 0), "ff6": (8, 0), "ff7": (9, 0), "down0": (2, 0), "down1": (10, 0), "down2": (11, 0), "down3": (12, 0), "upstream": (13, 0)}
FEED_PLAN = {"work": (4.9, 13), "down0": (4.9, 36), "down1": (1.5, 25), "down2": (1.8, 33), "down3": (1.2, 40)}
BACK_PLAN = {"tokens": (15.2, 0), "weights": (4.1, 1), "down0": (5.4, 4), "down1": (11.1, 9), "down2": (8.1, 19), "down3": (2.1, 0), "result": (9.7, 36), "ff0": (9.5, 0), "ff1": (5.8, 0), "ff2": (14.6, 4), "ff3": (7.3, 25), "ff4": (1.1, 18), "ff5": (3.7, 0), "ff6": (14.2, 21), "ff7": (0.3, 49), "out0": (13.7, 26), "out1": (5.5, 0)}
LEAVE_PLAN = {"tokens": (1.5, 0), "qkv0": (0.6, 55), "qkv2": (2, 24), "qkv1": (4.6, 47), "qkv3": (1.2, 9)}
BACKLOG = 12.0
LINK_TIME = {
    "s": {"s": 2 / 92e3},
    "zl": {"zl": 2 / 92e3},
    "y": {"y": 2 / 92e3},
    "zh": {"zh": 4 / 92e3, "zl": 2 / 92e3},
    "c": {"c": 1 / 300e3},
    "diagonal": {"s": 2 / 92e3, "zl": 2 / 92e3},
    "local": {"local": 1 / 1500e3},
}


class Lines:
    def __init__(self, send, recv, local):
        self.send, self.recv, self.local = send, recv, local
        self.sent, self.copied, self.traffic = [], 0, Traffic()

    def track(self, wait, source, link):
        size = int(np.prod(source.shape)) * jnp.dtype(source.dtype).itemsize
        return wait, self.traffic.start({name: time * size for name, time in LINK_TIME[link].items()})

    def push(self, source, target, device, link):
        at = len(self.sent)
        copy = pltpu.make_async_remote_copy(
            src_ref=source, dst_ref=target, send_sem=self.send.at[at], recv_sem=self.recv.at[at],
            device_id=device, device_id_type=MESH,
        )
        copy.start()
        self.sent.append(copy)
        return self.track(copy.wait_recv, source, link)

    def copy(self, source, target):
        copy = pltpu.make_async_copy(source, target, self.local.at[self.copied])
        copy.start()
        self.copied += 1
        return self.track(copy.wait, source, "local")

    def finish(self):
        for copy in self.sent:
            copy.wait_send()


def run(lines, works, plan, start=3.0):
    traffic, now = lines.traffic, start
    open_works, late, plan = [], None, dict(plan)

    def add(label, work):
        rank, begin = plan.get(label, (0.0, 0.0))
        open_works.append([rank, begin, work, next(work)])
        open_works.sort(key=lambda entry: entry[0])

    for work in works:
        if isinstance(work, list):
            late = work
        else:
            add(*work)
    while open_works:
        traffic.advance(now)
        for entry in open_works:
            waits, cost, link = entry[3]
            arrived = all(transfer["done"] is not None and transfer["done"] <= now for _, transfer in waits)
            if arrived and now >= entry[1] and (link is None or traffic.backlog(link) < BACKLOG):
                break
        else:
            now += 0.25
            continue
        for wait, _ in waits:
            wait()
        entry[1], entry[3] = 0.0, next(entry[2], None)
        now += cost + 0.15
        if entry[3] is None:
            open_works.remove(entry)
        while late:
            add(*late.pop(0))


def gather_team(lines, me, source, whole):
    yield [], 0, None
    mine, other = whole.at[me.zl, me.s], whole.at[1 - me.zl, me.s]
    across = lines.push(source, mine, me.at(zl=1 - me.zl), "zl")
    waits = [lines.copy(source, mine), lines.push(source, mine, me.at(s=1 - me.s), "s")]
    yield [across], 0, None
    waits.append(lines.push(other, other, me.at(s=1 - me.s), "s"))
    yield waits, 0, None


def gather_columns(lines, me, cut, whole, piece):
    other, start, size = piece
    s, columns = 1 - me.s if other else me.s, pl.ds(start, size)
    yield [], 0, "s"
    waits = []
    for flip in (0, 1):
        zl = 1 - me.zl if flip else me.zl
        for source, at in cut(s, zl, start, size):
            mine = whole.at[me.s, me.zh, me.zl, me.y, me.c, :, pl.ds(at, source.shape[1])]
            if other or flip:
                link = "diagonal" if other and flip else "s" if other else "zl"
                waits.append(lines.push(source, mine, me.at(s=s, zl=zl), link))
            else:
                waits.append(lines.copy(source, mine))
    yield waits, 0, "zh"
    part = whole.at[s, me.zh, :, me.y, me.c, :, columns]
    waits = [lines.push(part, part, me.at(zh=zh), "zh") for zh in me.highs()]
    yield waits, 0, "y"
    part = whole.at[s, :, :, me.y, me.c, :, columns]
    wait = lines.push(part, part, me.at(y=1 - me.y), "y")
    yield [wait], 0, None
    part = whole.at[s, :, :, :, me.c, :, columns]
    wait = lines.push(part, part, me.at(c=1 - me.c), "c")
    yield [wait], 0, None


def ready_cut(cut):
    return lambda s, zl, start, size: [(cut.at[s * 2 + zl, :, pl.ds(start, size)], start)]


def block_cut(zhs, shard, block):
    def cut(s, zl, start, size):
        found = []
        for at in range(start, start + size, block):
            number, zh = at // (zhs * block), at // block % zhs
            column = (number * 4 * zhs + (s * zhs + zh) * 2 + zl) * block
            found.append((shard.at[:, pl.ds(pl.multiple_of(column, block), block)], at))
        return found

    return cut


def swap_halves(left, right):
    width = left.shape[1]
    first = lax.broadcasted_iota(jnp.int32, (1, width), 1) < width // 2
    return (
        jnp.where(first, left, pltpu.roll(right, width // 2, 1)),
        jnp.where(first, pltpu.roll(left, width // 2, 1), right),
    )


def gather_rows(lines, me, source, whole, start, size):
    rows = pl.ds(start, size)
    yield [], 0, "zh"
    mine = whole.at[me.zh, me.y, me.c, rows]
    waits = [lines.copy(source.at[rows], mine)]
    waits += [lines.push(source.at[rows], mine, me.at(zh=zh), "zh") for zh in me.highs()]
    yield waits, 0, "y"
    part = whole.at[:, me.y, me.c, rows]
    wait = lines.push(part, part, me.at(y=1 - me.y), "y")
    yield [wait], 0, None
    part = whole.at[:, :, me.c, rows]
    wait = lines.push(part, part, me.at(c=1 - me.c), "c")
    yield [wait], 0, None


def add_into(target, sources, result=None):
    result = target if result is None else result

    def step(at, carry):
        rows = pl.ds(pl.multiple_of(at * ROWS, ROWS), ROWS)
        total = target[rows].astype(F32)
        for source in sources:
            total = total + source[rows].astype(F32)
        result[rows] = total.astype(result.dtype)
        return carry

    lax.fori_loop(0, target.shape[0] // ROWS, step, 0)


def add_time(*refs):
    return sum(int(np.prod(ref.shape)) for ref in refs) * ADD_TIME


ADD_TIME = 1.6e-6


def sum_columns(lines, me, grad, cut, buffers, piece):
    first, second, third = buffers
    other, start, size = piece
    s, columns = 1 - me.s if other else me.s, pl.ds(start, size)
    mine = grad.at[s, :, :, :, me.c, :, columns]
    yield [], 0, "c"
    wait = lines.push(grad.at[s, :, :, :, 1 - me.c, :, columns], first, me.at(c=1 - me.c), "c")
    yield [wait], add_time(first) / 2, "y"

    def fold(y):
        for zh in range(me.zhs):
            for zl in range(2):
                add_into(mine.at[zh, zl, y], [first.at[zh, zl, y]])

    fold(1 - me.y)
    wait = lines.push(mine.at[:, :, 1 - me.y], second, me.at(y=1 - me.y), "y")
    yield [], add_time(first) / 2, None
    fold(me.y)
    yield [wait], add_time(second), "zh"
    waits = []
    for step, zh in enumerate([*me.highs(), me.zh]):
        for zl in range(2):
            add_into(mine.at[zh, zl, me.y], [second.at[zh, zl]])
        if step < me.zhs - 1:
            waits.append(lines.push(mine.at[zh, :, me.y], third.at[step], me.at(zh=zh), "zh"))
    yield waits, add_time(third), None
    for zl in range(2):
        add_into(mine.at[me.zh, zl, me.y], [third.at[step, zl] for step in range(me.zhs - 1)])
    waits = []
    for flip in (0, 1):
        zl = 1 - me.zl if flip else me.zl
        source, target = mine.at[me.zh, zl, me.y], cut.at[me.s * 2 + me.zl, :, columns]
        if other or flip:
            link = "diagonal" if other and flip else "s" if other else "zl"
            waits.append(lines.push(source, target, me.at(s=s, zl=zl), link))
        else:
            waits.append(lines.copy(source, target))
    yield waits, 0, None


def sum_near(lines, me, grad, buffers, piece):
    first, second = buffers
    rows = pl.ds(*piece)
    mine = grad.at[:, :, me.c, rows]
    yield [], 0, "c"
    wait = lines.push(grad.at[:, :, 1 - me.c, rows], first, me.at(c=1 - me.c), "c")
    yield [wait], add_time(first) / 2, "y"
    for zh in range(me.zhs):
        add_into(mine.at[zh, 1 - me.y], [first.at[zh, 1 - me.y]])
    wait = lines.push(mine.at[:, 1 - me.y], second, me.at(y=1 - me.y), "y")
    yield [], add_time(first) / 2, None
    for zh in range(me.zhs):
        add_into(mine.at[zh, me.y], [first.at[zh, me.y]])
    yield [wait], add_time(second), None
    for zh in range(me.zhs):
        add_into(mine.at[zh, me.y], [second.at[zh]])


def sum_far(lines, me, part, total, buffers, piece):
    mine, third, final = buffers
    rows = pl.ds(*piece)
    yield [], 0, "zh"
    waits = [lines.copy(part.at[me.zh, rows], mine)]
    for step, zh in enumerate(me.highs()):
        waits.append(lines.push(part.at[zh, rows], third.at[step], me.at(zh=zh), "zh"))
    yield waits, add_time(third), None
    add_into(mine, [third.at[step] for step in range(me.zhs - 1)], final)
    wait = lines.copy(final, total.at[rows])
    yield [wait], 0, None


def sum_rows(lines, me, grad, total, near, far, piece):
    yield from sum_near(lines, me, grad, near, piece)
    yield from sum_far(lines, me, grad.at[:, me.y, me.c], total, far, piece)


def sum_team(lines, me, partial, own, passed, taken):
    first = [
        lines.copy(partial.at[1 - me.zl, me.s], passed),
        lines.push(partial.at[1 - me.zl, 1 - me.s], taken.at[0], me.at(s=1 - me.s), "s"),
    ]
    waits = [
        lines.push(partial.at[me.zl, 1 - me.s], taken.at[1], me.at(s=1 - me.s), "s"),
        lines.copy(partial.at[me.zl, me.s], own),
    ]
    yield first, add_time(passed), None
    add_into(passed, [taken.at[0]])
    waits.append(lines.push(passed, taken.at[2], me.at(zl=1 - me.zl), "zl"))
    yield waits, 3, None


def team_total(own, taken, rows):
    return own[rows].astype(F32) + taken[1, rows].astype(F32) + taken[2, rows].astype(F32)


def by_rows(count, body):
    def step(at, carry):
        body(pl.ds(pl.multiple_of(at * ROWS, ROWS), ROWS))
        return carry

    lax.fori_loop(0, count // ROWS, step, 0)


def row_pieces(size, parts):
    tiles, pieces, start = size // ROWS, [], 0
    for part in range(parts):
        count = (tiles * (part + 1) // parts - tiles * part // parts) * ROWS
        pieces.append((start, count))
        start += count
    return pieces


def column_pieces(columns, parts):
    lanes, pieces, start = columns // 128, [], 0
    for part in range(parts):
        size = (lanes * (part + 1) // parts - lanes * part // parts) * 128
        pieces.append((start, size))
        start += size
    return [(other, *piece) for other in (False, True) for piece in pieces]


def turn_pairs(values, tables, sign):
    return (
        values * tables[0]
        + pltpu.roll(values, 128 - ROTARY // 2, 1) * (tables[1] * sign)
        + pltpu.roll(values, ROTARY // 2, 1) * (tables[2] * sign)
    )


def rotary_tables(length):
    lane = np.arange(128) % HEAD_DIM
    halves = ROTARY // 2
    frequency = np.float32(10000.0) ** (np.float32(-2.0) * np.arange(halves, dtype=np.float32) / np.float32(ROTARY))
    angles = np.arange(length, dtype=np.float32)[:, None] * frequency[lane % halves][None, :]
    rotated = lane < ROTARY
    return np.stack([
        np.where(rotated, np.cos(angles), 1.0),
        np.where(lane < halves, -np.sin(angles), 0.0),
        np.where(rotated & (lane >= halves), np.sin(angles), 0.0),
    ]).astype(np.float32)


def lane_masks():
    lane = lax.broadcasted_iota(jnp.int32, (1, 128), 1)
    return [(lane < HEAD_DIM).astype(F32).astype(BF), (lane >= HEAD_DIM).astype(F32).astype(BF)], lane < HEAD_DIM


def softmax_rows(query, key):
    length = query.shape[0]
    scores = dot_nt(query, key) * 0.125
    below = lax.broadcasted_iota(jnp.int32, (length, length), 0) >= lax.broadcasted_iota(
        jnp.int32, (length, length), 1
    )
    scores = jnp.where(below, scores, -1e30)
    exponent = jnp.exp(scores - jnp.max(scores, axis=-1, keepdims=True))
    return exponent / jnp.sum(exponent, axis=-1, keepdims=True)


def pairs_of(seq, length, part, body):
    def step(at, carry):
        body(pl.ds(seq * length, length), pl.ds(pl.multiple_of(at * 128, 128), 128))
        return carry

    lax.fori_loop(0, part // 128, step, 0)


def forward_attention(first, weight, offset, tables, queries, keys, values, mixed):
    length, part = tables.shape[1], queries.shape[1]
    seqs = queries.shape[0] // length
    for number, target in enumerate((queries, keys, values)):
        for start in range(0, part, 256):
            at = number * part + start
            block = dot(first[...], weight[:, at : at + 256]) + offset[:, at : at + 256]
            if target is values:
                target[:, start : start + 256] = block.astype(BF)
                continue
            for seq in range(seqs):
                for lanes in range(0, 256, 128):
                    rows = slice(seq * length, (seq + 1) * length)
                    turned = turn_pairs(block[rows, lanes : lanes + 128], tables, 1.0)
                    target[rows, start + lanes : start + lanes + 128] = turned.astype(BF)
        yield [], 2.5 if number < 2 else 6, None

    masks, left = lane_masks()
    for seq in range(seqs):

        def body(rows, lanes):
            query, key, value = queries[rows, lanes], keys[rows, lanes], values[rows, lanes]
            sides = [dot(softmax_rows(query * mask, key).astype(BF), value) for mask in masks]
            mixed[rows, lanes] = jnp.where(left, *sides).astype(BF)

        pairs_of(seq, length, part, body)
        yield [], 6 if seq < seqs - 1 else 2, None


def backward_attention(grad_mixed, tables, queries, keys, values, grad_projected):
    length, part = tables.shape[1], queries.shape[1]
    seqs = queries.shape[0] // length
    masks, left = lane_masks()
    for seq in range(seqs):

        def body(rows, lanes):
            query, key, value = queries[rows, lanes], keys[rows, lanes], values[rows, lanes]
            grad = grad_mixed[rows, lanes]
            sides = []
            for mask in masks:
                probs = softmax_rows(query * mask, key)
                grad_probs = dot_nt(grad * mask, value)
                grad_scores = (
                    probs * (grad_probs - jnp.sum(probs * grad_probs, axis=-1, keepdims=True))
                ).astype(BF)
                sides.append((
                    dot(grad_scores, key) * 0.125,
                    dot_tn(grad_scores, query) * 0.125,
                    dot_tn(probs.astype(BF), grad),
                ))
            grads = [jnp.where(left, *pair).astype(BF) for pair in zip(*sides)]
            start = lanes.start
            for number, found in enumerate(grads):
                if number < 2:
                    found = turn_pairs(found.astype(F32), tables, -1.0).astype(BF)
                grad_projected[rows, pl.ds(pl.multiple_of(start + number * part, 128), 128)] = found

        pairs_of(seq, length, part, body)
        yield [], 9 if seq < seqs - 1 else 1, None


def enter_kernel(
    zhs, tokens, small, qkv, out, gate, up,
    tokens_all, small_all, qkv_all, out_all, gate_cut, up_cut, shard, cuts, send, recv, local,
):
    me, lines = Place(zhs), Lines(send, recv, local)
    loads = [lines.copy(gate, shard.at[0]), lines.copy(up, shard.at[1])]
    me.greet()
    block = qkv_all.shape[6] // 3 // zhs

    def cut_work():
        width = cuts.shape[3]
        kept = []
        for number, target in enumerate((gate_cut, up_cut)):
            yield loads if number == 0 else [], 2, None
            for s in range(2):
                at = 2 * s * width
                left = shard[number, :, at : at + width].astype(F32)
                right = shard[number, :, at + width : at + 2 * width].astype(F32)
                for zl, found in enumerate(swap_halves(left, right)):
                    cuts[number, s * 2 + zl] = found.astype(BF)
            kept.append(lines.copy(cuts.at[number], target))
        yield kept, 0, None

    run(lines, [
        *[("small", gather_columns(lines, me, ready_cut(small), small_all, (other, 0, 128))) for other in (False, True)],
        *[
            (f"qkv{at}", gather_columns(lines, me, block_cut(zhs, qkv, block), qkv_all, piece))
            for at, piece in enumerate(column_pieces(qkv_all.shape[6], QKV_GATHERS))
        ],
        *[
            (f"out{at}", gather_rows(lines, me, out, out_all, *piece))
            for at, piece in enumerate(row_pieces(out.shape[0], OUT_PARTS))
        ],
        ("tokens", gather_team(lines, me, tokens, tokens_all)),
        ("cut", cut_work()),
    ], ENTER_PLAN)
    lines.finish()


def middle_kernel(
    zhs, tokens, upstream, tokens_all, qkv_all, out_all, gate_cut, up_cut, down,
    first_gain, first_bias, offset, gain, bias, tables,
    middle, first_out, queries_out, keys_out, values_out, mixed_out,
    upstream_all, input_all, gate_all, up_all, down_all,
    whole, first, weight, out_weight, queries, keys, values, mixed, partial,
    own, passed, taken, second, send, recv, local,
):
    me, lines = Place(zhs), Lines(send, recv, local)
    loads = [lines.copy(tokens_all, whole), lines.copy(qkv_all, weight), lines.copy(out_all, out_weight)]
    me.greet()

    def tokens_work():
        yield loads[:1], 4, None

        def normed(rows):
            first[rows] = (norm_rows(whole[rows].astype(F32))[0] * first_gain[...] + first_bias[...]).astype(BF)

        by_rows(whole.shape[0], normed)
        yield loads[1:], 2.5, None
        yield from forward_attention(first, weight, offset, tables, queries, keys, values, mixed)
        for start in range(0, partial.shape[3], 512):
            block = dot(mixed[...], out_weight[:, start : start + 512])
            partial[:, :, :, start : start + 512] = block.astype(BF).reshape(partial.shape[:3] + (512,))
        yield from sum_team(lines, me, partial, own, passed, taken)

        def body(rows):
            values = tokens[rows].astype(F32) + team_total(own, taken, rows)
            middle[rows] = values
            second[rows] = (norm_rows(values)[0] * gain[...] + bias[...]).astype(BF)

        by_rows(middle.shape[0], body)
        kept = [
            lines.copy(source, target)
            for source, target in (
                (first, first_out), (queries, queries_out), (keys, keys_out), (values, values_out), (mixed, mixed_out),
            )
        ]
        yield from gather_team(lines, me, second, input_all)
        yield kept, 0, None

    rows = [gather_rows(lines, me, down, down_all, *piece) for piece in row_pieces(down.shape[0], DOWN_PARTS)]
    columns = [
        gather_columns(lines, me, ready_cut(cut), found, piece)
        for piece in column_pieces(gate_cut.shape[2], FF_PARTS)
        for cut, found in ((gate_cut, gate_all), (up_cut, up_all))
    ]
    run(lines, [
        ("tokens", tokens_work()),
        *[(f"ff{at}", work) for at, work in enumerate(columns)],
        *[(f"down{at}", work) for at, work in enumerate(rows)],
        ("upstream", gather_team(lines, me, upstream, upstream_all)),
    ], MIDDLE_PLAN)
    lines.finish()


def feed_kernel(
    zhs, input_all, upstream_all, gate_all, up_all, down_all,
    partial_down_out, partial_second_out, grad_gate_out, grad_up_out, down_part,
    second, upstream, gate_weight, up_weight, down_weight, gate, up, hidden, grad_gate, grad_up,
    partial_down, partial_second, grad_down, buffers, send, recv, local,
):
    me, lines = Place(zhs), Lines(send, recv, local)
    loads = [
        lines.copy(source, target)
        for source, target in (
            (input_all, second), (gate_all, gate_weight), (up_all, up_weight),
            (upstream_all, upstream), (down_all, down_weight),
        )
    ]
    me.greet()
    spawned, pieces = [], row_pieces(grad_down.shape[3], DOWN_PARTS)
    width, ff = gate_weight.shape
    tiles = [(start, min(256, ff - start)) for start in range(0, ff, 256)]

    def sums(piece, near):
        yield from sum_near(lines, me, grad_down, near, piece)
        rows = pl.ds(*piece)
        wait = lines.copy(grad_down.at[:, me.y, me.c, rows], down_part.at[:, rows])
        yield [wait], 0, None

    def work():
        yield loads[:3], 9, None
        for start, size in tiles:
            at = slice(start, start + size)
            gate_rows = dot(second[...], gate_weight[:, at])
            up_rows = dot(second[...], up_weight[:, at])
            gate[:, at], up[:, at] = gate_rows, up_rows
            hidden[:, at] = (gate_rows * jax.nn.sigmoid(gate_rows) * up_rows).astype(BF)
        yield loads[3:], 4.5, None
        for start in range(0, width, 512):
            block = dot_tn(hidden[...], upstream[:, start : start + 512]).astype(BF)
            grad_down[:, :, :, :, start : start + 512] = block.reshape(grad_down.shape[:4] + (512,))
        spawned.extend((f"down{at}", sums(piece, near)) for at, (piece, near) in enumerate(zip(pieces, buffers)))
        yield [], 5, None
        for start, size in tiles:
            at = slice(start, start + size)
            grad_hidden = dot_nt(upstream[...], down_weight[at])
            gate_rows = gate[:, at]
            sigmoid_gate = jax.nn.sigmoid(gate_rows)
            grad_gate[:, at] = (
                grad_hidden * up[:, at] * sigmoid_gate * (1.0 + gate_rows * (1.0 - sigmoid_gate))
            ).astype(BF)
            grad_up[:, at] = (grad_hidden * gate_rows * sigmoid_gate).astype(BF)
        waits = [lines.copy(grad_gate, grad_gate_out), lines.copy(grad_up, grad_up_out)]
        for start in range(0, width, 512):
            yield [], 2.5, None
            block = dot_nt(grad_gate[...], gate_weight[start : start + 512]) + dot_nt(
                grad_up[...], up_weight[start : start + 512]
            )
            partial_second[:, start : start + 512] = block.astype(BF)
        waits.append(lines.copy(partial_second, partial_second_out))
        for start in range(0, width, 1024):
            yield [], 2.5, None
            block = dot(hidden[...], down_weight[:, start : start + 1024])
            partial_down[:, start : start + 1024] = block.astype(BF)
        waits.append(lines.copy(partial_down, partial_down_out))
        yield waits, 0, None

    run(lines, [("work", work()), spawned], FEED_PLAN)
    lines.finish()


def back_kernel(
    zhs, middle, upstream, gain, partial_down, partial_second, down_part, input_all, gate_in, up_in,
    out_all, queries_in, keys_in, values_in, mixed_in, tables,
    result, grad_middle, sums, down_total, gate_total, up_total, out_total, projected_out, bias_sums,
    own_down, passed_down, taken_down, own_second, passed_second, taken_second, attended,
    attended_all, out_weight, queries, keys, values, mixed, grad_mixed, grad_projected, grad_out,
    second, grad_side, grad_gate, grad_up, cuts, joined, down_buffers, out_buffers, buffers, send, recv, local,
):
    me, lines = Place(zhs), Lines(send, recv, local)
    near_loads = [lines.copy(input_all, second), lines.copy(gate_in, grad_side)]
    loads = [
        lines.copy(source, target)
        for source, target in (
            (out_all, out_weight), (queries_in, queries), (keys_in, keys), (values_in, values), (mixed_in, mixed),
        )
    ]
    me.greet()
    spawned = []
    pieces = column_pieces(cuts.shape[3], FF_PARTS)

    def weights_work():
        number = 0
        for which, (grad, total) in enumerate(((grad_gate, gate_total), (grad_up, up_total))):
            yield near_loads if grad is grad_gate else [lines.copy(up_in, grad_side)], 4.5, None
            ff = grad_side.shape[1]
            for start in range(0, ff, 256):
                size = min(256, ff - start)
                block = dot_tn(second[...], grad_side[:, start : start + size]).astype(BF)
                grad[:, :, :, :, :, :, start : start + size] = block.reshape(grad.shape[:6] + (size,))
            left = list(pieces)
            for piece in pieces:
                work = piece_work(grad, which, total, buffers[number], piece, left)
                spawned.append((f"ff{number}", work))
                number += 1

    def piece_work(grad, which, total, found, piece, left):
        yield from sum_columns(lines, me, grad, cuts.at[which], found, piece)
        left.remove(piece)
        if not left:
            spawned.append(("join", join_work(which, total)))

    def join_work(which, total):
        yield [], 2, None
        width, kept = cuts.shape[3], []
        for s in range(2):
            sides = [cuts[which, s * 2 + zl].astype(F32) for zl in range(2)]
            for zh, found in enumerate(swap_halves(*sides)):
                joined[which, s * 2 + zh] = found
                at = (s * 2 + zh) * width
                kept.append(lines.copy(joined.at[which, s * 2 + zh], total.at[:, at : at + width]))
        yield kept, 0, None

    def tokens_work():
        yield [], 0, None
        yield from sum_team(lines, me, partial_second, own_second, passed_second, taken_second)
        sums[...] = jnp.zeros_like(sums)

        def body(rows):
            normed, scale_rows = norm_rows(middle[rows])
            grad = team_total(own_second, taken_second, rows)
            sums[0:1] += jnp.sum(grad * normed, axis=0, keepdims=True)
            sums[1:2] += jnp.sum(grad, axis=0, keepdims=True)
            grad = upstream[rows].astype(F32) + norm_back(grad * gain[...], normed, scale_rows)
            grad_middle[rows] = grad
            attended[rows] = grad.astype(BF)

        by_rows(middle.shape[0], body)
        yield from gather_team(lines, me, attended, attended_all)
        yield loads, 4, None
        count, width = mixed.shape[0], attended_all.shape[3]
        for start in range(0, width, 512):
            block = dot_tn(mixed[...], attended_all[:, :, :, start : start + 512].reshape(count, 512))
            grad_out[:, :, :, :, start : start + 512] = block.astype(BF).reshape(grad_out.shape[:4] + (512,))
        for at, piece in enumerate(row_pieces(out_total.shape[0], OUT_PARTS)):
            spawned.append((f"out{at}", sum_rows(lines, me, grad_out, out_total, *out_buffers[at], piece)))
        grad_mixed[...] = dot_nt(attended_all[...].reshape(count, width), out_weight[...]).astype(BF)
        yield [], 9, None
        yield from backward_attention(grad_mixed, tables, queries, keys, values, grad_projected)
        wait = lines.copy(grad_projected, projected_out)
        for start in range(0, grad_projected.shape[1], 256):
            block = jnp.sum(grad_projected[:, start : start + 256].astype(F32), axis=0, keepdims=True)
            bias_sums[:, start : start + 256] = block
        yield [wait], 0, None

    def result_work():
        yield [], 0, "s"
        yield from sum_team(lines, me, partial_down, own_down, passed_down, taken_down)

        def body(rows):
            result[rows] = (middle[rows] + team_total(own_down, taken_down, rows)).astype(BF)

        by_rows(middle.shape[0], body)

    far = [
        sum_far(lines, me, down_part, down_total, found, piece)
        for found, piece in zip(down_buffers, row_pieces(down_total.shape[0], DOWN_PARTS))
    ]
    run(lines, [
        ("tokens", tokens_work()),
        ("weights", weights_work()),
        *[(f"down{at}", work) for at, work in enumerate(far)],
        ("result", result_work()),
        spawned,
    ], BACK_PLAN)
    lines.finish()


def leave_kernel(
    zhs, tokens, grad_middle, gain, second_sums, bias_sums, grad_projected, first_in, qkv_in,
    grad_inputs, sums, qkv_total,
    first, weight, partial, grad_qkv, cut, own, passed, taken, steps, buffers, send, recv, local,
):
    me, lines = Place(zhs), Lines(send, recv, local)
    loads = [lines.copy(first_in, first), lines.copy(qkv_in, weight)]
    me.greet()

    spawned = []
    pieces = column_pieces(cut.shape[2], QKV_PARTS)
    left = list(pieces)

    def piece_work(at):
        yield from sum_columns(lines, me, grad_qkv, cut, buffers[at], pieces[at])
        left.remove(pieces[at])
        if not left:
            block = cut.shape[2] // 3 // zhs
            for s in range(2):
                for zl in range(2):
                    for start in range(0, cut.shape[2], block):
                        number, zh = start // (zhs * block), start // block % zhs
                        column = (number * 4 * zhs + (s * zhs + zh) * 2 + zl) * block
                        found = cut[s * 2 + zl, :, start : start + block]
                        qkv_total[:, column : column + block] = found.astype(F32)

    def tokens_work():
        yield loads, 3, None
        columns = grad_qkv.shape[6]
        for number in range(QKV_PARTS):
            _, start, size = pieces[number]
            for at in range(start, start + size, 256):
                block = dot_tn(first[...], grad_projected[:, at : at + 256]).astype(BF)
                grad_qkv[:, :, :, :, :, :, at : at + 256] = block.reshape(grad_qkv.shape[:6] + (256,))
            for at in (number, number + QKV_PARTS):
                spawned.append((f"qkv{at}", piece_work(at)))
            yield [], 3 if number < QKV_PARTS - 1 else 7, None
        for at in range(weight.shape[0] // 256):
            block = dot_nt(grad_projected[...], weight[at * 256 : at * 256 + 256])
            partial[:, :, :, at * 256 : at * 256 + 256] = block.astype(BF).reshape(partial.shape[:3] + (256,))
        yield from sum_team(lines, me, partial, own, passed, taken)
        steps[0] = jnp.zeros_like(steps[0])
        steps[0, 2:4] = second_sums[0:2]
        part = bias_sums.shape[1] // 3
        block = part // zhs
        for number in range(3):
            for zh in range(zhs):
                at = ((me.s * zhs + zh) * 2 + me.zl) * block
                steps[0, 4 + number : 5 + number, pl.ds(pl.multiple_of(at, 64), block)] = bias_sums[
                    :, number * part + zh * block : number * part + (zh + 1) * block
                ]

        def body(rows):
            normed, scale_rows = norm_rows(tokens[rows].astype(F32))
            grad = team_total(own, taken, rows)
            steps[0, 0:1] += jnp.sum(grad * normed, axis=0, keepdims=True)
            steps[0, 1:2] += jnp.sum(grad, axis=0, keepdims=True)
            grad_inputs[rows] = grad_middle[rows] + norm_back(grad * gain[...], normed, scale_rows)

        by_rows(tokens.shape[0], body)
        groups = [
            [me.at(s=1 - me.s)], [me.at(zl=1 - me.zl)], [me.at(c=1 - me.c)], [me.at(y=1 - me.y)],
            [me.at(zh=zh) for zh in me.highs()],
        ]
        at = 0
        for group, link in zip(groups, ("s", "zl", "c", "y", "zh")):
            arrived = [
                lines.push(steps.at[at], steps.at[at + 1 + number], device, link)
                for number, device in enumerate(group)
            ]
            yield arrived, 0.3, None
            total = steps[at]
            for number in range(len(group)):
                total = total + steps[at + 1 + number]
            at += len(group) + 1
            steps[at] = total
        sums[...] = steps[at]

    run(lines, [("tokens", tokens_work()), spawned], LEAVE_PLAN)
    lines.finish()


def near_buffers(zhs, size, width):
    return tuple(pltpu.VMEM(shape + (size, width), BF) for shape in ((zhs, 2), (zhs,)))


def far_buffers(zhs, size, width):
    return (
        pltpu.VMEM((size, width), BF), pltpu.VMEM((zhs - 1, size, width), BF), pltpu.VMEM((size, width), F32)
    )


def column_buffers(zhs, own, columns):
    return tuple(
        pltpu.VMEM(shape + (own, columns), BF) for shape in ((zhs, 2, 2), (zhs, 2), (zhs - 1, 2))
    )


IN_HBM = pl.BlockSpec(memory_space=pl.ANY)
IN_VMEM = pl.BlockSpec(memory_space=pltpu.VMEM)


def call(kernel, zhs, number, inputs, outputs, scratch, copies, locals_, limit):
    return pl.pallas_call(
        lambda *refs: kernel(zhs, *refs),
        out_shape=[jax.ShapeDtypeStruct(shape, kind) for shape, kind, _ in outputs],
        in_specs=[spec for _, spec in inputs],
        out_specs=[spec for _, _, spec in outputs],
        scratch_shapes=[
            *scratch,
            pltpu.SemaphoreType.DMA((copies,)),
            pltpu.SemaphoreType.DMA((copies,)),
            pltpu.SemaphoreType.DMA((locals_,)),
        ],
        compiler_params=pltpu.CompilerParams(
            collective_id=number, has_side_effects=True, vmem_limit_bytes=limit << 20
        ),
    )(*[array for array, _ in inputs])


def per_device(
    tokens, cotangent, norm1_gain, norm1_bias, qkv_weight, qkv_bias, out_weight,
    norm2_gain, norm2_bias, gate_weight, up_weight, down_weight,
):
    zh = lax.axis_size("zh")
    rows = tokens.shape[1]
    width = tokens.shape[2]
    own = qkv_weight.shape[0]
    ff = gate_weight.shape[1]
    ff_own = down_weight.shape[0]
    half = lax.axis_size("seq")
    length = rows * half
    seqs = lax.axis_size("zl")
    team = half * seqs
    part = width // team
    ff_part = ff // team
    devices = width // own
    tokens, cotangent = tokens[0], cotangent[0]
    index = (lax.axis_index("seq") * (devices // half)
             + ((lax.axis_index("zh") * 2 + lax.axis_index("zl")) * 2 + lax.axis_index("y")) * 2
             + lax.axis_index("c"))

    def mine_columns(whole, parts):
        block = whole.shape[0] // parts // (half * zh * seqs)
        cut = whole.reshape(parts, half, zh, seqs, block)
        cut = lax.dynamic_index_in_dim(cut, lax.axis_index("seq"), 1, keepdims=False)
        cut = lax.dynamic_index_in_dim(cut, lax.axis_index("zl"), 2, keepdims=False)
        return cut.reshape(-1)

    small = jnp.concatenate([norm1_gain, norm1_bias, norm2_gain, norm2_bias, qkv_bias]).astype(F32)
    small = jnp.pad(small, (0, 1024 - small.shape[0])).reshape(8, 128)
    small = jnp.broadcast_to(small, (team, 8, 128))
    token_shape = (seqs, half, rows, width)
    owners = (half, zh, seqs, 2, 2)
    count = team * rows
    limit = 60
    tables = rotary_tables(length)
    tokens_all, small_all, qkv_all, out_all, gate_cut, up_cut = call(
        enter_kernel, zh, 0,
        [
            (tokens, IN_HBM), (small, IN_HBM), (qkv_weight, IN_HBM), (out_weight, IN_HBM),
            (gate_weight, IN_HBM), (up_weight, IN_HBM),
        ],
        [
            (token_shape, BF, IN_HBM),
            (owners + (8, 128), F32, IN_HBM),
            (owners + (own, 3 * part), BF, IN_HBM),
            ((zh, 2, 2, own, width), BF, IN_HBM),
            ((team, own, ff_part), BF, IN_HBM),
            ((team, own, ff_part), BF, IN_HBM),
        ],
        [pltpu.VMEM((2, own, ff), BF), pltpu.VMEM((2, team, own, ff_part), BF)],
        3 + (2 + OUT_PARTS) * (zh + 4) + 2 * QKV_GATHERS * (3 * zh + 2), 32, 60,
    )
    small = small_all.reshape(devices, 1024)
    first_gain = small[:, :own].reshape(1, width)
    first_bias = small[:, own : 2 * own].reshape(1, width)
    second_gain = small[:, 2 * own : 3 * own].reshape(1, width)
    second_bias = small[:, 3 * own : 4 * own].reshape(1, width)
    qkv_offset = mine_columns(small[:, 4 * own : 7 * own].reshape(-1), 3).reshape(1, 3 * part)
    qkv_matrix = qkv_all.reshape(width, 3 * part)
    out_matrix = out_all.reshape(part, width)

    token_scratch = [
        pltpu.VMEM((rows, width), BF), pltpu.VMEM((rows, width), BF), pltpu.VMEM((3, rows, width), BF)
    ]
    head_shape = (count, part)
    heads = [(head_shape, BF, IN_HBM)] * 4
    head_scratch = [pltpu.VMEM(head_shape, BF)] * 4
    (
        middle, first_input, queries, keys, values, mixed, upstream_all, input_all, gate_all, up_all, down_all,
    ) = call(
        middle_kernel, zh, 1,
        [
            (tokens, IN_VMEM), (cotangent, IN_HBM), (tokens_all.reshape(count, width), IN_HBM),
            (qkv_matrix, IN_HBM), (out_matrix, IN_HBM),
            (gate_cut, IN_HBM), (up_cut, IN_HBM), (down_weight, IN_HBM),
            (first_gain, IN_VMEM), (first_bias, IN_VMEM), (qkv_offset, IN_VMEM),
            (second_gain, IN_VMEM), (second_bias, IN_VMEM), (tables, IN_VMEM),
        ],
        [
            ((rows, width), F32, IN_VMEM),
            ((count, width), BF, IN_HBM),
            *heads,
            (token_shape, BF, IN_HBM),
            (token_shape, BF, IN_HBM),
            (owners + (own, ff_part), BF, IN_HBM),
            (owners + (own, ff_part), BF, IN_HBM),
            ((zh, 2, 2, ff_own, width), BF, IN_HBM),
        ],
        [
            pltpu.VMEM((count, width), BF), pltpu.VMEM((count, width), BF),
            pltpu.VMEM((width, 3 * part), BF), pltpu.VMEM((part, width), BF),
            *head_scratch, pltpu.VMEM(token_shape, BF),
            *token_scratch, pltpu.VMEM((rows, width), BF),
        ],
        9 + (DOWN_PARTS + 4 * FF_PARTS) * (zh + 4), 40, limit,
    )
    second_input = input_all.reshape(count, width)
    ff_shape = (count, ff_part)
    down_pieces = [size for _, size in row_pieces(ff_own, DOWN_PARTS)]
    partial_down, partial_second, grad_gate, grad_up, down_part = call(
        feed_kernel, zh, 4,
        [
            (second_input, IN_HBM), (upstream_all.reshape(count, width), IN_HBM),
            (gate_all.reshape(width, ff_part), IN_HBM), (up_all.reshape(width, ff_part), IN_HBM),
            (down_all.reshape(ff_part, width), IN_HBM),
        ],
        [
            ((count, width), BF, IN_HBM),
            ((count, width), BF, IN_HBM),
            (ff_shape, BF, IN_HBM),
            (ff_shape, BF, IN_HBM),
            ((zh, ff_own, width), BF, IN_HBM),
        ],
        [
            pltpu.VMEM((count, width), BF), pltpu.VMEM((count, width), BF),
            pltpu.VMEM((width, ff_part), BF), pltpu.VMEM((width, ff_part), BF), pltpu.VMEM((ff_part, width), BF),
            pltpu.VMEM(ff_shape, F32), pltpu.VMEM(ff_shape, F32),
            *[pltpu.VMEM(ff_shape, BF)] * 3,
            pltpu.VMEM((count, width), BF), pltpu.VMEM((count, width), BF), pltpu.VMEM(down_all.shape, BF),
            [near_buffers(zh, size, width) for size in down_pieces],
        ],
        DOWN_PARTS * 2, 32, 60,
    )
    result, grad_middle, second_sums, down_total, gate_total, up_total, out_total, grad_projected, bias_sums = call(
        back_kernel, zh, 2,
        [
            (middle, IN_VMEM), (cotangent, IN_VMEM), (second_gain, IN_VMEM),
            (partial_down.reshape(token_shape), IN_HBM), (partial_second.reshape(token_shape), IN_HBM),
            (down_part, IN_HBM), (second_input, IN_HBM), (grad_gate, IN_HBM), (grad_up, IN_HBM),
            (out_matrix, IN_HBM), (queries, IN_HBM), (keys, IN_HBM), (values, IN_HBM), (mixed, IN_HBM),
            (tables, IN_VMEM),
        ],
        [
            ((rows, width), BF, IN_VMEM),
            ((rows, width), F32, IN_VMEM),
            ((8, width), F32, IN_VMEM),
            ((ff_own, width), F32, IN_HBM),
            ((own, ff), F32, IN_HBM),
            ((own, ff), F32, IN_HBM),
            ((own, width), F32, IN_HBM),
            ((count, 3 * part), BF, IN_HBM),
            ((1, 3 * part), F32, IN_VMEM),
        ],
        [
            *token_scratch, *token_scratch, pltpu.VMEM((rows, width), BF), pltpu.VMEM(token_shape, BF),
            pltpu.VMEM((part, width), BF), *head_scratch, pltpu.VMEM(head_shape, BF),
            pltpu.VMEM((count, 3 * part), BF), pltpu.VMEM(out_all.shape, BF),
            pltpu.VMEM((count, width), BF), pltpu.VMEM(ff_shape, BF),
            pltpu.VMEM(gate_all.shape, BF), pltpu.VMEM(gate_all.shape, BF),
            pltpu.VMEM((2, team, own, ff_part), BF), pltpu.VMEM((2, team, own, ff_part), F32),
            [far_buffers(zh, size, width) for size in down_pieces],
            [
                (near_buffers(zh, size, width), far_buffers(zh, size, width))
                for _, size in row_pieces(own, OUT_PARTS)
            ],
            [
                column_buffers(zh, own, size)
                for _ in range(2)
                for _, _, size in column_pieces(ff_part, FF_PARTS)
            ],
        ],
        9 + (OUT_PARTS + DOWN_PARTS + 4 * FF_PARTS) * (zh + 4), 60, 62,
    )
    grad_inputs, sums, qkv_total = call(
        leave_kernel, zh, 3,
        [
            (tokens, IN_VMEM), (grad_middle, IN_VMEM), (first_gain, IN_VMEM),
            (second_sums, IN_VMEM), (bias_sums, IN_VMEM), (grad_projected, IN_VMEM),
            (first_input, IN_HBM), (qkv_matrix, IN_HBM),
        ],
        [
            ((rows, width), F32, IN_VMEM),
            ((8, width), F32, IN_VMEM),
            ((own, 3 * width), F32, IN_VMEM),
        ],
        [
            pltpu.VMEM((count, width), BF), pltpu.VMEM((width, 3 * part), BF), pltpu.VMEM(token_shape, BF),
            pltpu.VMEM(qkv_all.shape, BF), pltpu.VMEM((team, own, 3 * part), BF),
            *token_scratch, pltpu.VMEM((zh + 9, 8, width), F32),
            [column_buffers(zh, own, size) for _, _, size in column_pieces(3 * part, QKV_PARTS)],
        ],
        zh + 6 + (2 * QKV_PARTS) * (zh + 4), 24, limit,
    )

    def mine(vector_row, size):
        return lax.dynamic_slice_in_dim(vector_row, index * size, size, 0)

    return (
        result[None],
        grad_inputs[None],
        mine(sums[0], own),
        mine(sums[1], own),
        qkv_total,
        mine(sums[4:7].reshape(-1), 3 * own),
        out_total,
        mine(sums[2], own),
        mine(sums[3], own),
        gate_total,
        up_total,
        down_total,
    )


def solution(mesh):
    half, shards = mesh.shape["seq"], mesh.shape["shard"]
    fine = jax.sharding.Mesh(mesh.devices.reshape(half, shards // 8, 2, 2, 2), ALL)
    token = P(("zh", "zl", "y", "c"), "seq", None)
    row = P(ALL)

    def program(*arguments):
        whole_tiles = shards == 16 and arguments[-1].shape[0] // (half * shards) % ROWS == 0
        return jax.shard_map(
            per_device if whole_tiles else plain_device,
            mesh=fine,
            in_specs=(token, token) + (row,) * 10,
            out_specs=(token, token) + (row,) * 10,
            check_vma=False,
        )(*arguments)

    return program
```

profile of v0, /device:TPU:0, one launch (start us, length us, event | category | flops | bytes accessed | tf_op | source)
XLA Modules:
  0.0 528.3 jit_solution(10607422343705348926)
XLA Ops:
  0.7 3.4 concatenate.3
  4.1 0.6 broadcast_in_dim.9.refs_1_
  4.7 82.8 %shard_map.220 = (bf16[2,2,160,2048]{3,2,1,0:T(8,128)(2,1)}, f32[2,2,2,2,2,8,128]{6,5,4,3,2,1,0:T(8,128)}, bf16[2,2,2,2,2,64,1536]{6,5,4,3,2,1,0:T(8,128)(2,1)},...) custom-call(bf16[160,2048]{1,0:T(8,128)(2,1)} %bitcast.37, ...), custom_call_target="tpu_custom_call" | custom-call | tf_op jit(solution)/shard_map/pallas_call | solution.py:1081
  87.5 0.9 copy.29
  88.4 0.1 fusion.4
  88.5 0.1 reshape_reshape.6
  88.6 0.6 constant_dynamic-slice_fusion.4
  89.2 0.7 reshape.94.refs_12_
  89.9 0.7 reshape.93.refs_11_.refs_2_
  90.6 0.7 reshape.91.refs_8_.refs_2_
  91.2 0.7 reshape.92.refs_9_
  91.9 138.9 %shard_map.221 = (f32[160,2048]{1,0:T(8,128)}, bf16[640,2048]{1,0:T(8,128)(2,1)}, bf16[640,512]{1,0:T(8,128)(2,1)}, bf16[640,512]{1,0:T(8,128)(2,1)}, bf16[640,5...) custom-call(bf16[160,2048]{1,0:T(8,128)(2,1)} %bitcast.38, ...), custom_call_target="tpu_custom_call" | custom-call | tf_op jit(solution)/shard_map/pallas_call | solution.py:1081
  230.8 57.7 %shard_map.222 = (bf16[640,2048]{1,0:T(8,128)(2,1)}, bf16[640,2048]{1,0:T(8,128)(2,1)}, bf16[640,1408]{1,0:T(8,128)(2,1)}, bf16[640,1408]{1,0:T(8,128)(2,1)}, bf16[2,176,2048]{2,1,0:T(8,128)(2,1)}) custom-call(bf16[640,2048]{1,0:T(8,128)(2,1)} %bitcast.33, bf16[640,2048]{1,0:T(8,128)(2,1)} %bitcast.48, bf16[2048,1408]{1,0:T(8,128)(2,1)} %bitcast.40, ...), custom_call_target="tpu_custom_call" | custom-call | tf_op jit(solution)/shard_map/pallas_call | solution.py:1081
  288.5 139.7 %shard_map.223 = (bf16[160,2048]{1,0:T(8,128)(2,1)}, f32[160,2048]{1,0:T(8,128)}, f32[8,2048]{1,0:T(8,128)}, f32[176,2048]{1,0:T(8,128)}, f32[64,5632]{1,0:T(8,1...) custom-call(f32[160,2048]{1,0:T(8,128)} %get-tuple-element.52.refs_0_, ...), custom_call_target="tpu_custom_call" | custom-call | tf_op jit(solution)/shard_map/pallas_call | solution.py:1081
  428.2 0.0 copy-start.5
  428.2 87.6 %shard_map.224 = (f32[160,2048]{1,0:T(8,128)}, f32[8,2048]{1,0:T(8,128)}, f32[64,6144]{1,0:T(8,128)}) custom-call(bf16[160,2048]{1,0:T(8,128)(2,1)} %bitcast.39, f32[160,2048]{1,0:T(8,128)} %get-tuple-element.68.refs_1_, f32[1,2048]{1,0:T(1,128)} %reshape.91.refs_8_.refs_2_, f32[8,2048]{1,0:T(8,128)} %get-tuple-element.69.refs_3_, ...), custom_call_target="tpu_custom_call" | custom-call | tf_op jit(solution)/shard_map/pallas_call | solution.py:1081
  515.8 0.0 copy-start.4
  515.8 1.0 slice.37
  516.8 1.0 fusion.5
  517.8 0.6 dynamic_slice.34
  518.5 0.6 fusion.2
  519.1 0.6 fusion
  519.7 0.0 copy-done.5
  519.7 0.0 copy-start
  519.7 0.8 copy.37
  520.5 0.0 copy-done.4
  520.5 1.1 copy.38
  521.6 0.0 copy-done
  521.6 0.0 copy-start.6
  521.6 0.0 copy-start.3
  521.6 1.1 copy.39
  522.7 0.2 copy-done.6
  522.9 0.0 copy-start.2
  522.9 0.8 copy.40
  523.7 0.0 copy-done.3
  523.7 1.1 copy.41
  524.8 0.0 copy-done.2
  524.8 0.0 copy-start.1
  524.8 1.1 copy.42
  525.9 0.8 copy-done.1
  526.7 1.1 copy.43
  (3 shorter events, 0.0 us)
Async XLA Ops:
  428.2 91.5 %copy-start.5 = (bf16[160,2048]{1,0:T(8,128)(2,1)S(1)}, bf16[160,2048]{1,0:T(8,128)(2,1)}, u32[]{:S(2)}) copy-start(bf16[160,2048]{1,0:T(8,128)(2,1)} %get-tuple-element.67) | copy-start | bytes 1966084
  515.8 4.7 copy-start.4
  519.7 1.9 copy-start
  521.6 1.4 copy-start.6
  521.6 2.2 copy-start.3
  522.9 1.9 copy-start.2
  524.8 1.9 copy-start.1
where the time goes:
time: 535 us; the launch traced here: 528 us
  Pallas kernels  507 us (95%)
  local copies, waits for them, and re-layouts  20.4 us (4%)
    pallas_call x5, Pallas kernels, call(): pl.pallas_call(lambda *refs: kernel(zhs, *refs), out_shape=[jax.ShapeDtyp...  507 us

commit v1 on v0

--- a/solution.py
+++ b/solution.py
@@ -256,10 +256,12 @@
         for step in range(1, self.zhs):
             yield (self.zh + step) % self.zhs
 
-    def greet(self):
+    def greet(self, corners=False):
         partners = [self.at(s=s, zl=zl) for s, zl in self.mates()]
         partners += [self.at(zh=zh) for zh in self.highs()]
         partners += [self.at(y=1 - self.y), self.at(c=1 - self.c)]
+        if corners:
+            partners += [self.at(zh=zh, y=1 - self.y) for zh in self.highs()]
         barrier = pltpu.get_barrier_semaphore()
         for partner in partners:
             pl.semaphore_signal(barrier, inc=1, device_id=partner, device_id_type=MESH)
@@ -301,11 +303,11 @@
 
 
 LATENCY = 2.0
-ENTER_PLAN = {"small": (7.8, 43), "qkv0": (4.3, 33), "qkv1": (10.8, 0), "qkv2": (6.1, 1), "qkv3": (10.6, 19), "qkv4": (3.8, 13), "qkv5": (11.5, 41), "out0": (2.2, 0), "out1": (2.6, 32), "tokens": (5.8, 13), "cut": (7, 0)}
-MIDDLE_PLAN = {"tokens": (0, 0), "ff0": (1, 0), "ff1": (3, 0), "ff2": (4, 0), "ff3": (5, 0), "ff4": (6, 0), "ff5": (7, 0), "ff6": (8, 0), "ff7": (9, 0), "down0": (2, 0), "down1": (10, 0), "down2": (11, 0), "down3": (12, 0), "upstream": (13, 0)}
-FEED_PLAN = {"work": (4.9, 13), "down0": (4.9, 36), "down1": (1.5, 25), "down2": (1.8, 33), "down3": (1.2, 40)}
-BACK_PLAN = {"tokens": (15.2, 0), "weights": (4.1, 1), "down0": (5.4, 4), "down1": (11.1, 9), "down2": (8.1, 19), "down3": (2.1, 0), "result": (9.7, 36), "ff0": (9.5, 0), "ff1": (5.8, 0), "ff2": (14.6, 4), "ff3": (7.3, 25), "ff4": (1.1, 18), "ff5": (3.7, 0), "ff6": (14.2, 21), "ff7": (0.3, 49), "out0": (13.7, 26), "out1": (5.5, 0)}
-LEAVE_PLAN = {"tokens": (1.5, 0), "qkv0": (0.6, 55), "qkv2": (2, 24), "qkv1": (4.6, 47), "qkv3": (1.2, 9)}
+ENTER_PLAN = {"small": (7.8, 43), "qkv0": (4.9, 33), "qkv1": (10.8, 0), "qkv2": (6.1, 1), "qkv3": (10.6, 19), "qkv4": (3.8, 13), "qkv5": (11.5, 41), "out0": (2.2, 0), "out1": (2.6, 32), "tokens": (5.8, 13), "cut": (2.3, 40), "backlog": 12}
+MIDDLE_PLAN = {"tokens": (0, 0), "ff0": (1, 0), "ff1": (3, 0), "ff2": (4, 0), "ff3": (5, 0), "ff4": (6, 0), "ff5": (7, 0), "ff6": (8, 0), "ff7": (9, 0), "down0": (2, 0), "down1": (10, 0), "down2": (11, 0), "down3": (12, 0), "upstream": (13, 8)}
+FEED_PLAN = {"work": (4.9, 0), "down0": (5.9, 0), "down1": (1, 0), "down2": (2.3, 35), "down3": (4.1, 43), "result": (1.3, 0)}
+BACK_PLAN = {"tokens": (16.9, 0), "weights": (17.1, 0), "down0": (12.9, 0), "down1": (7.6, 0), "down2": (12.3, 11), "down3": (0.2, 34), "ff0": (14.7, 49), "ff1": (12.6, 10), "ff2": (12.3, 29), "ff3": (3.9, 0), "ff4": (16, 0), "ff5": (6, 0), "ff6": (10.6, 61), "ff7": (9.2, 2), "out0": (6.2, 0), "out1": (16.3, 40), "join": (17.7, 21)}
+LEAVE_PLAN = {"weights": (4, 0), "tokens": (1.5, 0), "qkv0": (0.8, 24), "qkv2": (0.1, 0), "qkv1": (0.1, 33), "qkv3": (3.9, 19)}
 BACKLOG = 12.0
 LINK_TIME = {
     "s": {"s": 2 / 92e3},
@@ -351,6 +353,7 @@
 def run(lines, works, plan, start=3.0):
     traffic, now = lines.traffic, start
     open_works, late, plan = [], None, dict(plan)
+    limit = plan.get("backlog", BACKLOG)
 
     def add(label, work):
         rank, begin = plan.get(label, (0.0, 0.0))
@@ -367,7 +370,7 @@
         for entry in open_works:
             waits, cost, link = entry[3]
             arrived = all(transfer["done"] is not None and transfer["done"] <= now for _, transfer in waits)
-            if arrived and now >= entry[1] and (link is None or traffic.backlog(link) < BACKLOG):
+            if arrived and now >= entry[1] and (link is None or traffic.backlog(link) < limit):
                 break
         else:
             now += 0.25
@@ -556,22 +559,30 @@
 
 
 def sum_team(lines, me, partial, own, passed, taken):
-    first = [
-        lines.copy(partial.at[1 - me.zl, me.s], passed),
-        lines.push(partial.at[1 - me.zl, 1 - me.s], taken.at[0], me.at(s=1 - me.s), "s"),
-    ]
-    waits = [
-        lines.push(partial.at[me.zl, 1 - me.s], taken.at[1], me.at(s=1 - me.s), "s"),
-        lines.copy(partial.at[me.zl, me.s], own),
-    ]
-    yield first, add_time(passed), None
-    add_into(passed, [taken.at[0]])
+    load = lines.copy(partial.at[1 - me.zl, me.s], passed)
+    first = send_rows(lines, me, partial, taken, 1 - me.zl)
+    yield [load, first], add_time(passed), None
+    waits = [lines.copy(partial.at[me.zl, me.s], own), send_rows(lines, me, partial, taken, me.zl)]
+    add_into(passed, [taken.at[1 - me.zl]])
     waits.append(lines.push(passed, taken.at[2], me.at(zl=1 - me.zl), "zl"))
     yield waits, 3, None
 
 
-def team_total(own, taken, rows):
-    return own[rows].astype(F32) + taken[1, rows].astype(F32) + taken[2, rows].astype(F32)
+def send_rows(lines, me, partial, taken, zl):
+    return lines.push(partial.at[zl, 1 - me.s], taken.at[zl], me.at(s=1 - me.s), "s")
+
+
+def end_team(lines, me, partial, own, passed, taken, started):
+    load = lines.copy(partial.at[1 - me.zl, me.s], passed)
+    keep = lines.copy(partial.at[me.zl, me.s], own)
+    yield [load, *started], add_time(passed), None
+    add_into(passed, [taken.at[1 - me.zl]])
+    wait = lines.push(passed, taken.at[2], me.at(zl=1 - me.zl), "zl")
+    yield [keep, wait], 3, None
+
+
+def team_total(me, own, taken, rows):
+    return own[rows].astype(F32) + taken[me.zl, rows].astype(F32) + taken[2, rows].astype(F32)
 
 
 def by_rows(count, body):
@@ -645,7 +656,7 @@
     lax.fori_loop(0, part // 128, step, 0)
 
 
-def forward_attention(first, weight, offset, tables, queries, keys, values, mixed):
+def forward_attention(first, weight, offset, tables, queries, keys, values, mixed, leave):
     length, part = tables.shape[1], queries.shape[1]
     seqs = queries.shape[0] // length
     for number, target in enumerate((queries, keys, values)):
@@ -660,7 +671,7 @@
                     rows = slice(seq * length, (seq + 1) * length)
                     turned = turn_pairs(block[rows, lanes : lanes + 128], tables, 1.0)
                     target[rows, start + lanes : start + lanes + 128] = turned.astype(BF)
-        yield [], 2.5 if number < 2 else 6, None
+        yield [], 2.5 if number < 2 else 7, None
 
     masks, left = lane_masks()
     for seq in range(seqs):
@@ -671,7 +682,9 @@
             mixed[rows, lanes] = jnp.where(left, *sides).astype(BF)
 
         pairs_of(seq, length, part, body)
-        yield [], 6 if seq < seqs - 1 else 2, None
+        leave(seq)
+        if seq < seqs - 1:
+            yield [], 7, None
 
 
 def backward_attention(grad_mixed, tables, queries, keys, values, grad_projected):
@@ -765,14 +778,20 @@
 
         by_rows(whole.shape[0], normed)
         yield loads[1:], 2.5, None
-        yield from forward_attention(first, weight, offset, tables, queries, keys, values, mixed)
-        for start in range(0, partial.shape[3], 512):
-            block = dot(mixed[...], out_weight[:, start : start + 512])
-            partial[:, :, :, start : start + 512] = block.astype(BF).reshape(partial.shape[:3] + (512,))
-        yield from sum_team(lines, me, partial, own, passed, taken)
+        started = []
+
+        def leave(seq):
+            rows = slice(seq * tables.shape[1], (seq + 1) * tables.shape[1])
+            for start in range(0, partial.shape[3], 512):
+                block = dot(mixed[rows], out_weight[:, start : start + 512]).astype(BF)
+                partial[seq, :, :, start : start + 512] = block.reshape(partial.shape[1:3] + (512,))
+            started.append(send_rows(lines, me, partial, taken, seq))
+
+        yield from forward_attention(first, weight, offset, tables, queries, keys, values, mixed, leave)
+        yield from end_team(lines, me, partial, own, passed, taken, started)
 
         def body(rows):
-            values = tokens[rows].astype(F32) + team_total(own, taken, rows)
+            values = tokens[rows].astype(F32) + team_total(me, own, taken, rows)
             middle[rows] = values
             second[rows] = (norm_rows(values)[0] * gain[...] + bias[...]).astype(BF)
 
@@ -802,10 +821,10 @@
 
 
 def feed_kernel(
-    zhs, input_all, upstream_all, gate_all, up_all, down_all,
-    partial_down_out, partial_second_out, grad_gate_out, grad_up_out, down_part,
+    zhs, middle, input_all, upstream_all, gate_all, up_all, down_all,
+    result, partial_second_out, grad_gate_out, grad_up_out, down_part,
     second, upstream, gate_weight, up_weight, down_weight, gate, up, hidden, grad_gate, grad_up,
-    partial_down, partial_second, grad_down, buffers, send, recv, local,
+    partial_down, partial_second, grad_down, own, passed, taken, buffers, send, recv, local,
 ):
     me, lines = Place(zhs), Lines(send, recv, local)
     loads = [
@@ -839,6 +858,11 @@
             block = dot_tn(hidden[...], upstream[:, start : start + 512]).astype(BF)
             grad_down[:, :, :, :, start : start + 512] = block.reshape(grad_down.shape[:4] + (512,))
         spawned.extend((f"down{at}", sums(piece, near)) for at, (piece, near) in enumerate(zip(pieces, buffers)))
+        yield [], 4.5, None
+        for start in range(0, width, 512):
+            block = dot(hidden[...], down_weight[:, start : start + 512]).astype(BF)
+            partial_down[:, :, :, start : start + 512] = block.reshape(partial_down.shape[:3] + (512,))
+        spawned.append(("result", result_work()))
         yield [], 5, None
         for start, size in tiles:
             at = slice(start, start + size)
@@ -857,22 +881,25 @@
             )
             partial_second[:, start : start + 512] = block.astype(BF)
         waits.append(lines.copy(partial_second, partial_second_out))
-        for start in range(0, width, 1024):
-            yield [], 2.5, None
-            block = dot(hidden[...], down_weight[:, start : start + 1024])
-            partial_down[:, start : start + 1024] = block.astype(BF)
-        waits.append(lines.copy(partial_down, partial_down_out))
         yield waits, 0, None
+
+    def result_work():
+        yield from sum_team(lines, me, partial_down, own, passed, taken)
+
+        def body(rows):
+            result[rows] = (middle[rows] + team_total(me, own, taken, rows)).astype(BF)
+
+        by_rows(middle.shape[0], body)
 
     run(lines, [("work", work()), spawned], FEED_PLAN)
     lines.finish()
 
 
 def back_kernel(
-    zhs, middle, upstream, gain, partial_down, partial_second, down_part, input_all, gate_in, up_in,
+    zhs, middle, upstream, gain, partial_second, down_part, input_all, gate_in, up_in,
     out_all, queries_in, keys_in, values_in, mixed_in, tables,
-    result, grad_middle, sums, down_total, gate_total, up_total, out_total, projected_out, bias_sums,
-    own_down, passed_down, taken_down, own_second, passed_second, taken_second, attended,
+    grad_middle, sums, down_total, gate_total, up_total, out_total, projected_out, bias_sums,
+    own_second, passed_second, taken_second, attended,
     attended_all, out_weight, queries, keys, values, mixed, grad_mixed, grad_projected, grad_out,
     second, grad_side, grad_gate, grad_up, cuts, joined, down_buffers, out_buffers, buffers, send, recv, local,
 ):
@@ -927,7 +954,7 @@
 
         def body(rows):
             normed, scale_rows = norm_rows(middle[rows])
-            grad = team_total(own_second, taken_second, rows)
+            grad = team_total(me, own_second, taken_second, rows)
             sums[0:1] += jnp.sum(grad * normed, axis=0, keepdims=True)
             sums[1:2] += jnp.sum(grad, axis=0, keepdims=True)
             grad = upstream[rows].astype(F32) + norm_back(grad * gain[...], normed, scale_rows)
@@ -952,15 +979,6 @@
             bias_sums[:, start : start + 256] = block
         yield [wait], 0, None
 
-    def result_work():
-        yield [], 0, "s"
-        yield from sum_team(lines, me, partial_down, own_down, passed_down, taken_down)
-
-        def body(rows):
-            result[rows] = (middle[rows] + team_total(own_down, taken_down, rows)).astype(BF)
-
-        by_rows(middle.shape[0], body)
-
     far = [
         sum_far(lines, me, down_part, down_total, found, piece)
         for found, piece in zip(down_buffers, row_pieces(down_total.shape[0], DOWN_PARTS))
@@ -969,7 +987,6 @@
         ("tokens", tokens_work()),
         ("weights", weights_work()),
         *[(f"down{at}", work) for at, work in enumerate(far)],
-        ("result", result_work()),
         spawned,
     ], BACK_PLAN)
     lines.finish()
@@ -982,7 +999,7 @@
 ):
     me, lines = Place(zhs), Lines(send, recv, local)
     loads = [lines.copy(first_in, first), lines.copy(qkv_in, weight)]
-    me.greet()
+    me.greet(corners=True)
 
     spawned = []
     pieces = column_pieces(cut.shape[2], QKV_PARTS)
@@ -1001,17 +1018,18 @@
                         found = cut[s * 2 + zl, :, start : start + block]
                         qkv_total[:, column : column + block] = found.astype(F32)
 
-    def tokens_work():
-        yield loads, 3, None
-        columns = grad_qkv.shape[6]
+    def weights_work():
         for number in range(QKV_PARTS):
+            yield loads[:1] if number == 0 else [], 2.6, None
             _, start, size = pieces[number]
             for at in range(start, start + size, 256):
                 block = dot_tn(first[...], grad_projected[:, at : at + 256]).astype(BF)
                 grad_qkv[:, :, :, :, :, :, at : at + 256] = block.reshape(grad_qkv.shape[:6] + (256,))
             for at in (number, number + QKV_PARTS):
                 spawned.append((f"qkv{at}", piece_work(at)))
-            yield [], 3 if number < QKV_PARTS - 1 else 7, None
+
+    def tokens_work():
+        yield loads[1:], 5, None
         for at in range(weight.shape[0] // 256):
             block = dot_nt(grad_projected[...], weight[at * 256 : at * 256 + 256])
             partial[:, :, :, at * 256 : at * 256 + 256] = block.astype(BF).reshape(partial.shape[:3] + (256,))
@@ -1029,21 +1047,23 @@
 
         def body(rows):
             normed, scale_rows = norm_rows(tokens[rows].astype(F32))
-            grad = team_total(own, taken, rows)
+            grad = team_total(me, own, taken, rows)
             steps[0, 0:1] += jnp.sum(grad * normed, axis=0, keepdims=True)
             steps[0, 1:2] += jnp.sum(grad, axis=0, keepdims=True)
             grad_inputs[rows] = grad_middle[rows] + norm_back(grad * gain[...], normed, scale_rows)
 
         by_rows(tokens.shape[0], body)
+        others = [(zh, y) for y in (me.y, 1 - me.y) for zh in (me.zh, *me.highs())][1:]
         groups = [
-            [me.at(s=1 - me.s)], [me.at(zl=1 - me.zl)], [me.at(c=1 - me.c)], [me.at(y=1 - me.y)],
-            [me.at(zh=zh) for zh in me.highs()],
+            [(me.at(s=mate_s, zl=mate_zl), link) for (mate_s, mate_zl), link in zip(me.mates(), ("zl", "s", "diagonal"))],
+            [(me.at(zh=zh, y=y), "zh" if y is me.y else "y") for zh, y in others],
+            [(me.at(c=1 - me.c), "c")],
         ]
         at = 0
-        for group, link in zip(groups, ("s", "zl", "c", "y", "zh")):
+        for group in groups:
             arrived = [
                 lines.push(steps.at[at], steps.at[at + 1 + number], device, link)
-                for number, device in enumerate(group)
+                for number, (device, link) in enumerate(group)
             ]
             yield arrived, 0.3, None
             total = steps[at]
@@ -1053,7 +1073,7 @@
             steps[at] = total
         sums[...] = steps[at]
 
-    run(lines, [("tokens", tokens_work()), spawned], LEAVE_PLAN)
+    run(lines, [("weights", weights_work()), ("tokens", tokens_work()), spawned], LEAVE_PLAN)
     lines.finish()
 
 
@@ -1147,7 +1167,7 @@
             ((team, own, ff_part), BF, IN_HBM),
         ],
         [pltpu.VMEM((2, own, ff), BF), pltpu.VMEM((2, team, own, ff_part), BF)],
-        3 + (2 + OUT_PARTS) * (zh + 4) + 2 * QKV_GATHERS * (3 * zh + 2), 32, 60,
+        3 + (2 + OUT_PARTS) * (zh + 4) + DOWN_PARTS * zh + 2 * QKV_GATHERS * (3 * zh + 2), 32, 60,
     )
     small = small_all.reshape(devices, 1024)
     first_gain = small[:, :own].reshape(1, width)
@@ -1196,15 +1216,15 @@
     second_input = input_all.reshape(count, width)
     ff_shape = (count, ff_part)
     down_pieces = [size for _, size in row_pieces(ff_own, DOWN_PARTS)]
-    partial_down, partial_second, grad_gate, grad_up, down_part = call(
+    result, partial_second, grad_gate, grad_up, down_part = call(
         feed_kernel, zh, 4,
         [
-            (second_input, IN_HBM), (upstream_all.reshape(count, width), IN_HBM),
+            (middle, IN_VMEM), (second_input, IN_HBM), (upstream_all.reshape(count, width), IN_HBM),
             (gate_all.reshape(width, ff_part), IN_HBM), (up_all.reshape(width, ff_part), IN_HBM),
             (down_all.reshape(ff_part, width), IN_HBM),
         ],
         [
-            ((count, width), BF, IN_HBM),
+            ((rows, width), BF, IN_VMEM),
             ((count, width), BF, IN_HBM),
             (ff_shape, BF, IN_HBM),
             (ff_shape, BF, IN_HBM),
@@ -1215,22 +1235,21 @@
             pltpu.VMEM((width, ff_part), BF), pltpu.VMEM((width, ff_part), BF), pltpu.VMEM((ff_part, width), BF),
             pltpu.VMEM(ff_shape, F32), pltpu.VMEM(ff_shape, F32),
             *[pltpu.VMEM(ff_shape, BF)] * 3,
-            pltpu.VMEM((count, width), BF), pltpu.VMEM((count, width), BF), pltpu.VMEM(down_all.shape, BF),
-            [near_buffers(zh, size, width) for size in down_pieces],
-        ],
-        DOWN_PARTS * 2, 32, 60,
-    )
-    result, grad_middle, second_sums, down_total, gate_total, up_total, out_total, grad_projected, bias_sums = call(
+            pltpu.VMEM(token_shape, BF), pltpu.VMEM((count, width), BF), pltpu.VMEM(down_all.shape, BF),
+            *token_scratch, [near_buffers(zh, size, width) for size in down_pieces],
+        ],
+        3 + DOWN_PARTS * 2, 32, 62,
+    )
+    grad_middle, second_sums, down_total, gate_total, up_total, out_total, grad_projected, bias_sums = call(
         back_kernel, zh, 2,
         [
             (middle, IN_VMEM), (cotangent, IN_VMEM), (second_gain, IN_VMEM),
-            (partial_down.reshape(token_shape), IN_HBM), (partial_second.reshape(token_shape), IN_HBM),
+            (partial_second.reshape(token_shape), IN_HBM),
             (down_part, IN_HBM), (second_input, IN_HBM), (grad_gate, IN_HBM), (grad_up, IN_HBM),
             (out_matrix, IN_HBM), (queries, IN_HBM), (keys, IN_HBM), (values, IN_HBM), (mixed, IN_HBM),
             (tables, IN_VMEM),
         ],
         [
-            ((rows, width), BF, IN_VMEM),
             ((rows, width), F32, IN_VMEM),
             ((8, width), F32, IN_VMEM),
             ((ff_own, width), F32, IN_HBM),
@@ -1241,7 +1260,7 @@
             ((1, 3 * part), F32, IN_VMEM),
         ],
         [
-            *token_scratch, *token_scratch, pltpu.VMEM((rows, width), BF), pltpu.VMEM(token_shape, BF),
+            *token_scratch, pltpu.VMEM((rows, width), BF), pltpu.VMEM(token_shape, BF),
             pltpu.VMEM((part, width), BF), *head_scratch, pltpu.VMEM(head_shape, BF),
             pltpu.VMEM((count, 3 * part), BF), pltpu.VMEM(out_all.shape, BF),
             pltpu.VMEM((count, width), BF), pltpu.VMEM(ff_shape, BF),
@@ -1275,10 +1294,10 @@
         [
             pltpu.VMEM((count, width), BF), pltpu.VMEM((width, 3 * part), BF), pltpu.VMEM(token_shape, BF),
             pltpu.VMEM(qkv_all.shape, BF), pltpu.VMEM((team, own, 3 * part), BF),
-            *token_scratch, pltpu.VMEM((zh + 9, 8, width), F32),
+            *token_scratch, pltpu.VMEM((2 * zh + 8, 8, width), F32),
             [column_buffers(zh, own, size) for _, _, size in column_pieces(3 * part, QKV_PARTS)],
         ],
-        zh + 6 + (2 * QKV_PARTS) * (zh + 4), 24, limit,
+        2 * zh + 8 + (2 * QKV_PARTS) * (zh + 4), 24, limit,
     )
 
     def mine(vector_row, size):

time: 535 us -> 524 us (0.979)
  Pallas kernels: 507 us -> 496 us
    pallas_call x5, Pallas kernels: 507 us -> 496 us  [call(): pl.pallas_call(lambda *refs: kernel(zhs, *refs), out_shape=[jax.ShapeDtyp...]
where the time goes in v1:
time: 524 us; the launch traced here: 518 us
  Pallas kernels  496 us (95%)
  local copies, waits for them, and re-layouts  20.4 us (4%)
    pallas_call x5, Pallas kernels, call(): pl.pallas_call(lambda *refs: kernel(zhs, *refs), out_shape=[jax.ShapeDtyp...  496 us

profile of v1, /device:TPU:0, one launch (start us, length us, event | category | flops | bytes accessed | tf_op | source)
XLA Modules:
  0.0 517.5 jit_solution(11479558884415780949)
XLA Ops:
  0.7 3.4 concatenate.3
  4.1 0.6 broadcast_in_dim.9.refs_1_
  4.7 81.1 %shard_map.220 = (bf16[2,2,160,2048]{3,2,1,0:T(8,128)(2,1)}, f32[2,2,2,2,2,8,128]{6,5,4,3,2,1,0:T(8,128)}, bf16[2,2,2,2,2,64,1536]{6,5,4,3,2,1,0:T(8,128)(2,1)},...) custom-call(bf16[160,2048]{1,0:T(8,128)(2,1)} %bitcast.36, ...), custom_call_target="tpu_custom_call" | custom-call | tf_op jit(solution)/shard_map/pallas_call | solution.py:1101
  85.9 0.9 copy.29
  86.8 0.1 fusion.4
  86.9 0.1 reshape_reshape.6
  87.0 0.6 constant_dynamic-slice_fusion.4
  87.6 0.7 reshape.91.refs_12_
  88.3 0.7 reshape.90.refs_11_.refs_2_
  88.9 0.7 reshape.88.refs_8_.refs_2_
  89.6 0.7 reshape.89.refs_9_
  90.3 128.4 %shard_map.221 = (f32[160,2048]{1,0:T(8,128)}, bf16[640,2048]{1,0:T(8,128)(2,1)}, bf16[640,512]{1,0:T(8,128)(2,1)}, bf16[640,512]{1,0:T(8,128)(2,1)}, bf16[640,5...) custom-call(bf16[160,2048]{1,0:T(8,128)(2,1)} %bitcast.37, ...), custom_call_target="tpu_custom_call" | custom-call | tf_op jit(solution)/shard_map/pallas_call | solution.py:1101
  218.7 60.3 %shard_map.222 = (bf16[160,2048]{1,0:T(8,128)(2,1)}, bf16[640,2048]{1,0:T(8,128)(2,1)}, bf16[640,1408]{1,0:T(8,128)(2,1)}, bf16[640,1408]{1,0:T(8,128)(2,1)}, bf16[2,176,2048]{2,1,0:T(8,128)(2,1)}) custom-call(f32[160,2048]{1,0:T(8,128)} %get-tuple-element.51.refs_0_, bf16[640,2048]{1,0:T(8,128)(2,1)} %bitcast.32, bf16[640,2048]{1,0:T(8,128)(2,1)} %bitcast.44, ...), custom_call_target="tpu_custom_call" | custom-call | tf_op jit(solution)/shard_map/pallas_call | solution.py:1101
  278.9 137.4 %shard_map.223 = (f32[160,2048]{1,0:T(8,128)}, f32[8,2048]{1,0:T(8,128)}, f32[176,2048]{1,0:T(8,128)}, f32[64,5632]{1,0:T(8,128)}, f32[64,5632]{1,0:T(8,128)}, /...) custom-call(f32[160,2048]{1,0:T(8,128)} %get-tuple-element.51.refs_0_, ...), custom_call_target="tpu_custom_call" | custom-call | tf_op jit(solution)/shard_map/pallas_call | solution.py:1101
  416.4 0.0 copy-start.5
  416.4 88.7 %shard_map.224 = (f32[160,2048]{1,0:T(8,128)}, f32[8,2048]{1,0:T(8,128)}, f32[64,6144]{1,0:T(8,128)}) custom-call(bf16[160,2048]{1,0:T(8,128)(2,1)} %bitcast.38, f32[160,2048]{1,0:T(8,128)} %get-tuple-element.66.refs_1_, f32[1,2048]{1,0:T(1,128)} %reshape.88.refs_8_.refs_2_, f32[8,2048]{1,0:T(8,128)} %get-tuple-element.67.refs_3_, ...), custom_call_target="tpu_custom_call" | custom-call | tf_op jit(solution)/shard_map/pallas_call | solution.py:1101
  505.1 0.0 copy-start.4
  505.1 1.0 slice.37
  506.1 1.0 fusion.5
  507.1 0.6 dynamic_slice.34
  507.7 0.6 fusion.2
  508.3 0.6 fusion
  508.9 0.0 copy-done.5
  508.9 0.0 copy-start
  508.9 0.8 copy.37
  509.8 0.0 copy-done.4
  509.8 1.1 copy.38
  510.8 0.0 copy-done
  510.8 0.0 copy-start.6
  510.8 0.0 copy-start.3
  510.8 1.1 copy.39
  512.0 0.2 copy-done.6
  512.2 0.0 copy-start.2
  512.2 0.8 copy.40
  513.0 0.0 copy-done.3
  513.0 1.1 copy.41
  514.1 0.0 copy-done.2
  514.1 0.0 copy-start.1
  514.1 1.1 copy.42
  515.2 0.8 copy-done.1
  516.0 1.1 copy.43
  (3 shorter events, 0.0 us)
Async XLA Ops:
  416.4 92.6 %copy-start.5 = (bf16[160,2048]{1,0:T(8,128)(2,1)S(1)}, bf16[160,2048]{1,0:T(8,128)(2,1)}, u32[]{:S(2)}) copy-start(bf16[160,2048]{1,0:T(8,128)(2,1)} %get-tuple-element.57) | copy-start | bytes 1966084
  505.1 4.7 copy-start.4
  508.9 1.9 copy-start
  510.8 1.4 copy-start.6
  510.8 2.2 copy-start.3
  512.2 1.9 copy-start.2
  514.1 1.9 copy-start.1

commit v2 on v1

--- a/solution.py
+++ b/solution.py
@@ -307,7 +307,7 @@
 MIDDLE_PLAN = {"tokens": (0, 0), "ff0": (1, 0), "ff1": (3, 0), "ff2": (4, 0), "ff3": (5, 0), "ff4": (6, 0), "ff5": (7, 0), "ff6": (8, 0), "ff7": (9, 0), "down0": (2, 0), "down1": (10, 0), "down2": (11, 0), "down3": (12, 0), "upstream": (13, 8)}
 FEED_PLAN = {"work": (4.9, 0), "down0": (5.9, 0), "down1": (1, 0), "down2": (2.3, 35), "down3": (4.1, 43), "result": (1.3, 0)}
 BACK_PLAN = {"tokens": (16.9, 0), "weights": (17.1, 0), "down0": (12.9, 0), "down1": (7.6, 0), "down2": (12.3, 11), "down3": (0.2, 34), "ff0": (14.7, 49), "ff1": (12.6, 10), "ff2": (12.3, 29), "ff3": (3.9, 0), "ff4": (16, 0), "ff5": (6, 0), "ff6": (10.6, 61), "ff7": (9.2, 2), "out0": (6.2, 0), "out1": (16.3, 40), "join": (17.7, 21)}
-LEAVE_PLAN = {"weights": (4, 0), "tokens": (1.5, 0), "qkv0": (0.8, 24), "qkv2": (0.1, 0), "qkv1": (0.1, 33), "qkv3": (3.9, 19)}
+LEAVE_PLAN = {"weights": (4, 0), "tokens": (1.5, 0), "qkv0": (0.8, 24), "qkv2": (0.1, 0), "qkv1": (0.1, 33), "qkv3": (3.9, 19), "backlog": 7}
 BACKLOG = 12.0
 LINK_TIME = {
     "s": {"s": 2 / 92e3},
@@ -464,15 +464,17 @@
 def add_into(target, sources, result=None):
     result = target if result is None else result
 
+    size = 2 * ROWS if target.shape[0] % (2 * ROWS) == 0 else ROWS
+
     def step(at, carry):
-        rows = pl.ds(pl.multiple_of(at * ROWS, ROWS), ROWS)
+        rows = pl.ds(pl.multiple_of(at * size, size), size)
         total = target[rows].astype(F32)
         for source in sources:
             total = total + source[rows].astype(F32)
         result[rows] = total.astype(result.dtype)
         return carry
 
-    lax.fori_loop(0, target.shape[0] // ROWS, step, 0)
+    lax.fori_loop(0, target.shape[0] // size, step, 0)
 
 
 def add_time(*refs):
@@ -743,7 +745,7 @@
         yield kept, 0, None
 
     run(lines, [
-        *[("small", gather_columns(lines, me, ready_cut(small), small_all, (other, 0, 128))) for other in (False, True)],
+        *[("small", gather_columns(lines, me, lambda *_: [(small, 0)], small_all, (other, 0, 128))) for other in (False, True)],
         *[
             (f"qkv{at}", gather_columns(lines, me, block_cut(zhs, qkv, block), qkv_all, piece))
             for at, piece in enumerate(column_pieces(qkv_all.shape[6], QKV_GATHERS))
@@ -1144,9 +1146,11 @@
         cut = lax.dynamic_index_in_dim(cut, lax.axis_index("zl"), 2, keepdims=False)
         return cut.reshape(-1)
 
-    small = jnp.concatenate([norm1_gain, norm1_bias, norm2_gain, norm2_bias, qkv_bias]).astype(F32)
-    small = jnp.pad(small, (0, 1024 - small.shape[0])).reshape(8, 128)
-    small = jnp.broadcast_to(small, (team, 8, 128))
+    small, at = jnp.zeros((1024,), F32), 0
+    for vector in (norm1_gain, norm1_bias, norm2_gain, norm2_bias, qkv_bias):
+        small += jnp.pad(vector.astype(F32), (at, 1024 - at - vector.shape[0]))
+        at += vector.shape[0]
+    small = small.reshape(8, 128)
     token_shape = (seqs, half, rows, width)
     owners = (half, zh, seqs, 2, 2)
     count = team * rows

time: 524 us -> 521 us (level)
  no operation moved by 1% of the time
where the time goes in v2:
time: 521 us; the launch traced here: 515 us
  Pallas kernels  496 us (95%)
  local copies, waits for them, and re-layouts  16.4 us (3%)
    pallas_call x5, Pallas kernels, call(): pl.pallas_call(lambda *refs: kernel(zhs, *refs), out_shape=[jax.ShapeDtyp...  496 us

profile of v2, /device:TPU:0, one launch (start us, length us, event | category | flops | bytes accessed | tf_op | source)
XLA Modules:
  0.0 514.5 jit_solution(11892503162616472774)
XLA Ops:
  0.7 1.4 add_bitcast_fusion.refs_1_
  2.1 81.1 %shard_map.220 = (bf16[2,2,160,2048]{3,2,1,0:T(8,128)(2,1)}, f32[2,2,2,2,2,8,128]{6,5,4,3,2,1,0:T(8,128)}, bf16[2,2,2,2,2,64,1536]{6,5,4,3,2,1,0:T(8,128)(2,1)},...) custom-call(bf16[160,2048]{1,0:T(8,128)(2,1)} %bitcast.35, ...), custom_call_target="tpu_custom_call" | custom-call | tf_op jit(solution)/shard_map/pallas_call | solution.py:1103
  83.2 0.9 copy.29
  84.1 0.1 fusion.4
  84.2 0.1 reshape_reshape.6
  84.3 0.6 constant_dynamic-slice_fusion.4
  84.9 0.7 reshape.87.refs_12_
  85.6 0.7 reshape.86.refs_11_.refs_2_
  86.3 0.7 reshape.84.refs_8_.refs_2_
  87.0 0.7 reshape.85.refs_9_
  87.6 128.3 %shard_map.221 = (f32[160,2048]{1,0:T(8,128)}, bf16[640,2048]{1,0:T(8,128)(2,1)}, bf16[640,512]{1,0:T(8,128)(2,1)}, bf16[640,512]{1,0:T(8,128)(2,1)}, bf16[640,5...) custom-call(bf16[160,2048]{1,0:T(8,128)(2,1)} %bitcast.36, ...), custom_call_target="tpu_custom_call" | custom-call | tf_op jit(solution)/shard_map/pallas_call | solution.py:1103
  215.9 60.1 %shard_map.222 = (bf16[160,2048]{1,0:T(8,128)(2,1)}, bf16[640,2048]{1,0:T(8,128)(2,1)}, bf16[640,1408]{1,0:T(8,128)(2,1)}, bf16[640,1408]{1,0:T(8,128)(2,1)}, bf16[2,176,2048]{2,1,0:T(8,128)(2,1)}) custom-call(f32[160,2048]{1,0:T(8,128)} %get-tuple-element.51.refs_0_, bf16[640,2048]{1,0:T(8,128)(2,1)} %bitcast.31, bf16[640,2048]{1,0:T(8,128)(2,1)} %bitcast.43, ...), custom_call_target="tpu_custom_call" | custom-call | tf_op jit(solution)/shard_map/pallas_call | solution.py:1103
  276.1 137.7 %shard_map.223 = (f32[160,2048]{1,0:T(8,128)}, f32[8,2048]{1,0:T(8,128)}, f32[176,2048]{1,0:T(8,128)}, f32[64,5632]{1,0:T(8,128)}, f32[64,5632]{1,0:T(8,128)}, /...) custom-call(f32[160,2048]{1,0:T(8,128)} %get-tuple-element.51.refs_0_, ...), custom_call_target="tpu_custom_call" | custom-call | tf_op jit(solution)/shard_map/pallas_call | solution.py:1103
  413.8 0.0 copy-start.5
  413.8 88.3 %shard_map.224 = (f32[160,2048]{1,0:T(8,128)}, f32[8,2048]{1,0:T(8,128)}, f32[64,6144]{1,0:T(8,128)}) custom-call(bf16[160,2048]{1,0:T(8,128)(2,1)} %bitcast.37, f32[160,2048]{1,0:T(8,128)} %get-tuple-element.66.refs_1_, f32[1,2048]{1,0:T(1,128)} %reshape.84.refs_8_.refs_2_, f32[8,2048]{1,0:T(8,128)} %get-tuple-element.67.refs_3_, ...), custom_call_target="tpu_custom_call" | custom-call | tf_op jit(solution)/shard_map/pallas_call | solution.py:1103
  502.1 0.0 copy-start.4
  502.1 1.0 slice.37
  503.0 1.0 fusion.5
  504.1 0.6 dynamic_slice.34
  504.7 0.6 fusion.2
  505.3 0.6 fusion
  505.9 0.0 copy-done.5
  505.9 0.0 copy-start
  505.9 0.8 copy.37
  506.7 0.0 copy-done.4
  506.7 1.1 copy.38
  507.8 0.0 copy-done
  507.8 0.0 copy-start.6
  507.8 0.0 copy-start.3
  507.8 1.1 copy.39
  509.0 0.2 copy-done.6
  509.2 0.0 copy-start.2
  509.2 0.8 copy.40
  510.0 0.0 copy-done.3
  510.0 1.1 copy.41
  511.1 0.0 copy-done.2
  511.1 0.0 copy-start.1
  511.1 1.1 copy.42
  512.2 0.8 copy-done.1
  513.0 1.1 copy.43
  (2 shorter events, 0.0 us)
Async XLA Ops:
  413.8 92.1 %copy-start.5 = (bf16[160,2048]{1,0:T(8,128)(2,1)S(1)}, bf16[160,2048]{1,0:T(8,128)(2,1)}, u32[]{:S(2)}) copy-start(bf16[160,2048]{1,0:T(8,128)(2,1)} %get-tuple-element.57) | copy-start | bytes 1966084
  502.1 4.7 copy-start.4
  505.9 1.9 copy-start
  507.8 1.4 copy-start.6
  507.8 2.2 copy-start.3
  509.2 1.9 copy-start.2
  511.1 1.9 copy-start.1

commit v3 on v2

--- a/solution.py
+++ b/solution.py
@@ -762,13 +762,14 @@
 
 def middle_kernel(
     zhs, tokens, upstream, tokens_all, qkv_all, out_all, gate_cut, up_cut, down,
-    first_gain, first_bias, offset, gain, bias, tables,
+    norms, offset, tables,
     middle, first_out, queries_out, keys_out, values_out, mixed_out,
     upstream_all, input_all, gate_all, up_all, down_all,
     whole, first, weight, out_weight, queries, keys, values, mixed, partial,
     own, passed, taken, second, send, recv, local,
 ):
     me, lines = Place(zhs), Lines(send, recv, local)
+    first_gain, first_bias, gain, bias = (norms.at[row : row + 1] for row in range(4))
     loads = [lines.copy(tokens_all, whole), lines.copy(qkv_all, weight), lines.copy(out_all, out_weight)]
     me.greet()
 
@@ -898,7 +899,7 @@
 
 
 def back_kernel(
-    zhs, middle, upstream, gain, partial_second, down_part, input_all, gate_in, up_in,
+    zhs, middle, upstream, norms, partial_second, down_part, input_all, gate_in, up_in,
     out_all, queries_in, keys_in, values_in, mixed_in, tables,
     grad_middle, sums, down_total, gate_total, up_total, out_total, projected_out, bias_sums,
     own_second, passed_second, taken_second, attended,
@@ -906,6 +907,7 @@
     second, grad_side, grad_gate, grad_up, cuts, joined, down_buffers, out_buffers, buffers, send, recv, local,
 ):
     me, lines = Place(zhs), Lines(send, recv, local)
+    gain = norms.at[2:3]
     near_loads = [lines.copy(input_all, second), lines.copy(gate_in, grad_side)]
     loads = [
         lines.copy(source, target)
@@ -995,11 +997,12 @@
 
 
 def leave_kernel(
-    zhs, tokens, grad_middle, gain, second_sums, bias_sums, grad_projected, first_in, qkv_in,
+    zhs, tokens, grad_middle, norms, second_sums, bias_sums, grad_projected, first_in, qkv_in,
     grad_inputs, sums, qkv_total,
     first, weight, partial, grad_qkv, cut, own, passed, taken, steps, buffers, send, recv, local,
 ):
     me, lines = Place(zhs), Lines(send, recv, local)
+    gain = norms.at[0:1]
     loads = [lines.copy(first_in, first), lines.copy(qkv_in, weight)]
     me.greet(corners=True)
 
@@ -1174,10 +1177,7 @@
         3 + (2 + OUT_PARTS) * (zh + 4) + DOWN_PARTS * zh + 2 * QKV_GATHERS * (3 * zh + 2), 32, 60,
     )
     small = small_all.reshape(devices, 1024)
-    first_gain = small[:, :own].reshape(1, width)
-    first_bias = small[:, own : 2 * own].reshape(1, width)
-    second_gain = small[:, 2 * own : 3 * own].reshape(1, width)
-    second_bias = small[:, 3 * own : 4 * own].reshape(1, width)
+    norms = small[:, : 4 * own].reshape(devices, 4, own).transpose(1, 0, 2).reshape(4, width)
     qkv_offset = mine_columns(small[:, 4 * own : 7 * own].reshape(-1), 3).reshape(1, 3 * part)
     qkv_matrix = qkv_all.reshape(width, 3 * part)
     out_matrix = out_all.reshape(part, width)
@@ -1196,8 +1196,7 @@
             (tokens, IN_VMEM), (cotangent, IN_HBM), (tokens_all.reshape(count, width), IN_HBM),
             (qkv_matrix, IN_HBM), (out_matrix, IN_HBM),
             (gate_cut, IN_HBM), (up_cut, IN_HBM), (down_weight, IN_HBM),
-            (first_gain, IN_VMEM), (first_bias, IN_VMEM), (qkv_offset, IN_VMEM),
-            (second_gain, IN_VMEM), (second_bias, IN_VMEM), (tables, IN_VMEM),
+            (norms, IN_VMEM), (qkv_offset, IN_VMEM), (tables, IN_VMEM),
         ],
         [
             ((rows, width), F32, IN_VMEM),
@@ -1247,7 +1246,7 @@
     grad_middle, second_sums, down_total, gate_total, up_total, out_total, grad_projected, bias_sums = call(
         back_kernel, zh, 2,
         [
-            (middle, IN_VMEM), (cotangent, IN_VMEM), (second_gain, IN_VMEM),
+            (middle, IN_VMEM), (cotangent, IN_VMEM), (norms, IN_VMEM),
             (partial_second.reshape(token_shape), IN_HBM),
             (down_part, IN_HBM), (second_input, IN_HBM), (grad_gate, IN_HBM), (grad_up, IN_HBM),
             (out_matrix, IN_HBM), (queries, IN_HBM), (keys, IN_HBM), (values, IN_HBM), (mixed, IN_HBM),
@@ -1286,7 +1285,7 @@
     grad_inputs, sums, qkv_total = call(
         leave_kernel, zh, 3,
         [
-            (tokens, IN_VMEM), (grad_middle, IN_VMEM), (first_gain, IN_VMEM),
+            (tokens, IN_VMEM), (grad_middle, IN_VMEM), (norms, IN_VMEM),
             (second_sums, IN_VMEM), (bias_sums, IN_VMEM), (grad_projected, IN_VMEM),
             (first_input, IN_HBM), (qkv_matrix, IN_HBM),
         ],

time: 521 us -> 519 us (level)
  no operation moved by 1% of the time
where the time goes in v3:
time: 519 us; the launch traced here: 512 us
  Pallas kernels  495 us (95%)
  local copies, waits for them, and re-layouts  14.4 us (3%)
    pallas_call x5, Pallas kernels, call(): pl.pallas_call(lambda *refs: kernel(zhs, *refs), out_shape=[jax.ShapeDtyp...  495 us

profile of v3, /device:TPU:0, one launch (start us, length us, event | category | flops | bytes accessed | tf_op | source)
XLA Modules:
  0.0 512.4 jit_solution(16002315265161020116)
XLA Ops:
  0.7 1.4 add_bitcast_fusion.refs_1_
  2.1 81.1 %shard_map.220 = (bf16[2,2,160,2048]{3,2,1,0:T(8,128)(2,1)}, f32[2,2,2,2,2,8,128]{6,5,4,3,2,1,0:T(8,128)}, bf16[2,2,2,2,2,64,1536]{6,5,4,3,2,1,0:T(8,128)(2,1)},...) custom-call(bf16[160,2048]{1,0:T(8,128)(2,1)} %bitcast.36, ...), custom_call_target="tpu_custom_call" | custom-call | tf_op jit(solution)/shard_map/pallas_call | solution.py:1106
  83.2 0.9 copy.28
  84.2 0.1 reshape_reshape.6
  84.3 0.6 constant_dynamic-slice_fusion.4
  84.9 0.1 reshape.78
  85.0 0.7 reshape.79.refs_8_.refs_2_
  85.7 128.3 %shard_map.221 = (f32[160,2048]{1,0:T(8,128)}, bf16[640,2048]{1,0:T(8,128)(2,1)}, bf16[640,512]{1,0:T(8,128)(2,1)}, bf16[640,512]{1,0:T(8,128)(2,1)}, bf16[640,5...) custom-call(bf16[160,2048]{1,0:T(8,128)(2,1)} %bitcast.37, ...), custom_call_target="tpu_custom_call" | custom-call | tf_op jit(solution)/shard_map/pallas_call | solution.py:1106
  214.0 60.1 %shard_map.222 = (bf16[160,2048]{1,0:T(8,128)(2,1)}, bf16[640,2048]{1,0:T(8,128)(2,1)}, bf16[640,1408]{1,0:T(8,128)(2,1)}, bf16[640,1408]{1,0:T(8,128)(2,1)}, bf16[2,176,2048]{2,1,0:T(8,128)(2,1)}) custom-call(f32[160,2048]{1,0:T(8,128)} %get-tuple-element.51.refs_0_, bf16[640,2048]{1,0:T(8,128)(2,1)} %bitcast.32, bf16[640,2048]{1,0:T(8,128)(2,1)} %bitcast.44, ...), custom_call_target="tpu_custom_call" | custom-call | tf_op jit(solution)/shard_map/pallas_call | solution.py:1106
  274.1 137.7 %shard_map.223 = (f32[160,2048]{1,0:T(8,128)}, f32[8,2048]{1,0:T(8,128)}, f32[176,2048]{1,0:T(8,128)}, f32[64,5632]{1,0:T(8,128)}, f32[64,5632]{1,0:T(8,128)}, /...) custom-call(f32[160,2048]{1,0:T(8,128)} %get-tuple-element.51.refs_0_, ...), custom_call_target="tpu_custom_call" | custom-call | tf_op jit(solution)/shard_map/pallas_call | solution.py:1106
  411.8 0.0 copy-start.5
  411.8 88.2 %shard_map.224 = (f32[160,2048]{1,0:T(8,128)}, f32[8,2048]{1,0:T(8,128)}, f32[64,6144]{1,0:T(8,128)}) custom-call(bf16[160,2048]{1,0:T(8,128)(2,1)} %bitcast.38, f32[160,2048]{1,0:T(8,128)} %get-tuple-element.66.refs_1_, f32[4,2048]{1,0:T(4,128)} %reshape.79.refs_8_.refs_2_, f32[8,2048]{1,0:T(8,128)} %get-tuple-element.67.refs_3_, ...), custom_call_target="tpu_custom_call" | custom-call | tf_op jit(solution)/shard_map/pallas_call | solution.py:1106
  500.0 0.0 copy-start.4
  500.0 1.0 slice.25
  500.9 1.0 fusion.4
  502.0 0.6 dynamic_slice.34
  502.6 0.6 fusion.2
  503.2 0.6 fusion
  503.8 0.0 copy-done.5
  503.8 0.0 copy-start
  503.8 0.8 copy.36
  504.6 0.0 copy-done.4
  504.6 1.1 copy.37
  505.7 0.0 copy-done
  505.7 0.0 copy-start.6
  505.7 0.0 copy-start.3
  505.7 1.1 copy.38
  506.8 0.2 copy-done.6
  507.1 0.0 copy-start.2
  507.1 0.8 copy.39
  507.9 0.0 copy-done.3
  507.9 1.1 copy.40
  509.0 0.0 copy-done.2
  509.0 0.0 copy-start.1
  509.0 1.1 copy.41
  510.1 0.8 copy-done.1
  510.8 1.1 copy.42
  (4 shorter events, 0.0 us)
Async XLA Ops:
  411.8 92.0 %copy-start.5 = (bf16[160,2048]{1,0:T(8,128)(2,1)S(1)}, bf16[160,2048]{1,0:T(8,128)(2,1)}, u32[]{:S(2)}) copy-start(bf16[160,2048]{1,0:T(8,128)(2,1)} %get-tuple-element.57) | copy-start | bytes 1966084
  500.0 4.7 copy-start.4
  503.8 1.9 copy-start
  505.7 1.4 copy-start.6
  505.7 2.2 copy-start.3
  507.1 1.9 copy-start.2
  509.0 1.9 copy-start.1
